TPU v7x, 256 devices: a whole 4x4x8 slice. The times are simulated.
256 devices in a mesh: sp: 16 (over z_lo, y, core), tp: 4 (over x), dp: 4 (over z_hi).
Axes of the slice: x: 4, y: 4, z: 8 (z_hi: 4, z_lo: 2; z = z_hi * 2 + z_lo), core: 2. Of those that a mesh axis runs over, the one named last changes fastest.
Arguments:
- queries: bfloat16 [16, 16, 32, 4096], P('dp', 'sp', 'tp'), parts along dimension 0
- key_proj: bfloat16 [16, 16, 32, 4096], P('dp', 'sp', 'tp'), parts along dimension 0
- values: bfloat16 [16, 16, 32, 4096], P('dp', 'sp', 'tp'), parts along dimension 0, may hold values from -6 to 6
- hidden_in: bfloat16 [16, 16, 32, 5120], P('dp', 'sp', 'tp'), parts along dimension 0, may hold values from -6 to 6
- out_weight: bfloat16 [4096, 5120], P('sp', 'tp'), may hold values from -0.09375 to 0.09375
- out_gate: float32 [5120], replicated, may hold values from 0.1 to 1.9
- mod_shift: float32 [5120], replicated, may hold values from -3 to 3
- mod_scale: float32 [5120], replicated, may hold values from -0.5 to 0.5
- head_weight: bfloat16 [5120, 64], replicated, may hold values from -0.078125 to 0.078125
- conv_first: bfloat16 [432, 384], replicated, may hold values from -0.3125 to 0.3125
- bias_first: float32 [384], replicated, may hold values from -3 to 3
- norm_gain: float32 [384], replicated, may hold values from 0.1 to 1.9
- conv_second: bfloat16 [10368, 384], replicated, may hold values from -0.0625 to 0.0625
- bias_second: float32 [384], replicated, may hold values from -3 to 3
Outputs:
- block_out: bfloat16 [16, 16, 32, 5120], P('dp', 'sp', 'tp'), parts along dimension 0
- decoded: bfloat16 [16, 32, 64, 384], P('dp', 'sp', 'tp'), parts along dimension 0
There are 4 independent parts, one for each index of `dp`. A program takes and returns all parts, laid end to end along the dimension named above; an argument that names none is the same for every part. Nothing has to cross between parts.
All inputs are finite; a program needn't handle non-finite values.
Results may differ from a plain program's by a relative error of at most 0.02.
Values may be sent and summed in bfloat16 or wider, within the bound.
No kernel may reach another device: no remote copies, remote signals or barrier semaphores. Data moves between devices by JAX's collectives and lax.ppermute only.
A program may use at most 64 MiB of HBM per device.

v0:
```python
import jax
import jax.numpy as jnp
from jax import lax
from jax.sharding import PartitionSpec as P

HEAD_DIM = 128


def padded_2(block, sides, width):
    for axis, dim in sides:
        count = lax.axis_size(axis)
        forward = [(i, i + 1) for i in range(count - 1)]
        backward = [(target, source) for source, target in forward]
        low = lax.ppermute(
            lax.slice_in_dim(block, block.shape[dim] - width, None, axis=dim), axis, forward
        )
        high = lax.ppermute(lax.slice_in_dim(block, 0, width, axis=dim), axis, backward)
        block = jnp.concatenate([low, block, high], axis=dim)
    return block


def group_attention(query_group, key_group, value_group, block_rows):
    count, heads, width = query_group.shape
    blocks = query_group.reshape(-1, block_rows, heads, width)

    def one_block(block_queries):
        scores = jnp.einsum(
            "qhd,khd->hqk", block_queries, key_group, preferred_element_type=jnp.float32
        ) * HEAD_DIM ** (-0.5)
        row_max = jnp.max(scores, axis=2, keepdims=True)
        expo_terms = jnp.exp(scores - row_max)
        totals = jnp.sum(expo_terms, axis=2)
        mixed = jnp.einsum(
            "hqk,khd->qhd",
            expo_terms.astype(jnp.bfloat16),
            value_group,
            preferred_element_type=jnp.float32,
        )
        return (mixed / jnp.transpose(totals)[:, :, None]).astype(jnp.bfloat16)

    return lax.map(one_block, blocks).reshape(count, heads * width)


def causal_conv(padded, weight):
    frames = padded.shape[0] - 2
    height = padded.shape[1] - 2
    span_cols = padded.shape[2] - 2
    taps = [
        padded[t : t + frames, i : i + height, j : j + span_cols, :]
        for t in range(3)
        for i in range(3)
        for j in range(3)
    ]
    stacked = jnp.concatenate(taps, axis=-1)
    flat_rows = stacked.reshape(-1, stacked.shape[-1])
    return jnp.dot(flat_rows, weight, preferred_element_type=jnp.float32).reshape(
        frames, height, span_cols, weight.shape[1]
    )


def time_pad(grid):
    return jnp.pad(grid, ((2, 0), (0, 0), (0, 0), (0, 0)))


def activate(first, norm_gain):
    wide = first.astype(jnp.float32)
    square_mean = jnp.mean(wide * wide, axis=-1, keepdims=True)
    normed = wide * lax.rsqrt(square_mean + 1e-06) * norm_gain
    return jax.nn.silu(normed).astype(jnp.bfloat16)


def shards(
    queries,
    key_proj,
    values,
    hidden_in,
    out_weight,
    out_gate,
    mod_shift,
    mod_scale,
    head_weight,
    conv_first,
    bias_first,
    norm_gain,
    conv_second,
    bias_second,
):
    local_queries, local_keys, local_values = (
        lax.all_to_all(queries, "sp", split_axis=3, concat_axis=1, tiled=True),
        lax.all_to_all(key_proj, "sp", split_axis=3, concat_axis=1, tiled=True),
        lax.all_to_all(values, "sp", split_axis=3, concat_axis=1, tiled=True),
    )
    all_keys, all_values = (
        lax.all_gather(local_keys, "tp", axis=2, tiled=True),
        lax.all_gather(local_values, "tp", axis=2, tiled=True),
    )
    frames, rows, cols_dev, group_width = local_queries.shape
    heads_here = group_width // HEAD_DIM
    frame_rows = rows * cols_dev
    per_block = max(1, min(frames, 512 // frame_rows))
    while frames % per_block != 0:
        per_block = per_block - 1
    block_rows = per_block * frame_rows
    query_group = local_queries.reshape(-1, heads_here, HEAD_DIM)
    key_group = all_keys.reshape(-1, heads_here, HEAD_DIM)
    value_group = all_values.reshape(-1, heads_here, HEAD_DIM)
    attended = group_attention(query_group, key_group, value_group, block_rows)
    terms = jnp.dot(
        attended,
        lax.all_gather(out_weight, "tp", axis=1, tiled=True),
        preferred_element_type=jnp.float32,
    )
    terms = terms.reshape(frames, rows, cols_dev, terms.shape[1])
    projected = lax.psum_scatter(
        terms.astype(jnp.bfloat16), "sp", scatter_dimension=1, tiled=True
    ).astype(jnp.float32)
    block_out = (hidden_in.astype(jnp.float32) + out_gate * projected).astype(jnp.bfloat16)
    stream = block_out.astype(jnp.float32)
    row_mean = jnp.mean(stream, axis=-1, keepdims=True)
    centred = stream - row_mean
    variance = jnp.mean(centred * centred, axis=-1, keepdims=True)
    modded = (centred * lax.rsqrt(variance + 1e-06) * (1.0 + mod_scale) + mod_shift).astype(
        jnp.bfloat16
    )
    row_dev = hidden_in.shape[1]
    lat_ch = head_weight.shape[1] // 4
    patch = jnp.dot(
        modded.reshape(-1, modded.shape[-1]), head_weight, preferred_element_type=jnp.float32
    ).astype(jnp.bfloat16)
    patch = patch.reshape(frames, row_dev, cols_dev, 2, 2, lat_ch)
    latent = patch.transpose(0, 1, 3, 2, 4, 5).reshape(frames, 2 * row_dev, 2 * cols_dev, lat_ch)
    grown = padded_2(latent, (("sp", 1), ("tp", 2)), 1)
    first = (causal_conv(time_pad(grown), conv_first) + bias_first).astype(jnp.bfloat16)
    active = activate(first, norm_gain)
    grown_active = padded_2(active, (("sp", 1), ("tp", 2)), 1)
    second = causal_conv(time_pad(grown_active), conv_second)
    decoded = (first.astype(jnp.float32) + second + bias_second).astype(jnp.bfloat16)
    return (block_out, decoded)


def solution(mesh):
    in_specs = (
        P("dp", "sp", "tp", None),
        P("dp", "sp", "tp", None),
        P("dp", "sp", "tp", None),
        P("dp", "sp", "tp", None),
        P("sp", "tp"),
        P(),
        P(),
        P(),
        P(),
        P(),
        P(),
        P(),
        P(),
        P(),
    )
    out_specs = (P("dp", "sp", "tp", None), P("dp", "sp", "tp", None))
    return jax.shard_map(shards, mesh=mesh, in_specs=in_specs, out_specs=out_specs, check_vma=False)
```

profile of v0, /device:TPU:38, one launch (start us, length us, event | category | flops | bytes accessed | tf_op | source)
XLA Modules:
  0.0 339.7 jit_solution(539492446816590818)
XLA Ops:
  7.2 5.6 %copy.55 = bf16[4,1,8,4096]{2,0,1,3:T(4,128)(2,1)} copy(bf16[4,1,8,4096]{3,2,1,0:T(8,128)(2,1)} %param.16) | data formatting | bytes 524288 | tf_op args[2]
  12.9 5.8 %reshape.93 = bf16[16,2,4096]{2,1,0:T(2,128)(2,1)S(1)} reshape(bf16[4096,1,4,8]{3,2,1,0:T(4,128)(2,1)} %bitcast.70) | data formatting | bytes 524288
  18.6 12.5 %all_to_all.51 = bf16[16,2,4096]{2,1,0:T(2,128)(2,1)S(1)} all-to-all(bf16[16,2,4096]{2,1,0:T(2,128)(2,1)S(1)} %reshape.93), channel_id=1, replica_groups=mesh['sp'=16,'tp'=4,'dp'=4] {'sp'}, dimensions={0} | all-to-all | bytes 524288 | tf_op jit(solution)/shard_map/all_to_all | solution.py:91
  31.2 5.9 %reshape.94 = bf16[4096,1,4,8]{3,2,1,0:T(4,128)(2,1)} reshape(bf16[16,2,4096]{2,1,0:T(2,128)(2,1)S(1)} %all_to_all.51) | data formatting | bytes 524288
  37.1 5.2 %copy.67 = bf16[4,1,8,16,256]{4,3,2,0,1:T(8,128)(2,1)} copy(bf16[4,1,8,16,256]{2,0,4,3,1:T(4,128)(2,1)} %bitcast.67) | data formatting | bytes 524288 | tf_op jit(solution)/shard_map/all_to_all | solution.py:91
  42.4 4.6 %copy.50 = bf16[4,1,8,4096]{2,0,1,3:T(4,128)(2,1)} copy(bf16[4,1,8,4096]{3,2,1,0:T(8,128)(2,1)S(1)} %copy-done.5) | data formatting | bytes 524288 | tf_op args[1]
  46.9 5.8 %reshape.95 = bf16[16,2,4096]{2,1,0:T(2,128)(2,1)S(1)} reshape(bf16[4096,1,4,8]{3,2,1,0:T(4,128)(2,1)} %bitcast.71) | data formatting | bytes 524288
  52.7 10.6 %all_to_all.52 = bf16[16,2,4096]{2,1,0:T(2,128)(2,1)S(1)} all-to-all(bf16[16,2,4096]{2,1,0:T(2,128)(2,1)S(1)} %reshape.95), channel_id=1, replica_groups=mesh['sp'=16,'tp'=4,'dp'=4] {'sp'}, dimensions={0} | all-to-all | bytes 524288 | tf_op jit(solution)/shard_map/all_to_all | solution.py:90
  63.3 5.9 %reshape.96 = bf16[4096,1,4,8]{3,2,1,0:T(4,128)(2,1)} reshape(bf16[16,2,4096]{2,1,0:T(2,128)(2,1)S(1)} %all_to_all.52) | data formatting | bytes 524288
  69.2 5.2 %copy.66 = bf16[4,1,8,16,256]{4,3,2,0,1:T(8,128)(2,1)} copy(bf16[4,1,8,16,256]{2,0,4,3,1:T(4,128)(2,1)} %bitcast.68) | data formatting | bytes 524288 | tf_op jit(solution)/shard_map/all_to_all | solution.py:90
  75.2 4.6 %copy.47 = bf16[4,1,8,4096]{2,0,1,3:T(4,128)(2,1)} copy(bf16[4,1,8,4096]{3,2,1,0:T(8,128)(2,1)S(1)} %copy-done.6) | data formatting | bytes 524288 | tf_op args[0]
  79.8 5.8 %reshape.97 = bf16[16,2,4096]{2,1,0:T(2,128)(2,1)S(1)} reshape(bf16[4096,1,4,8]{3,2,1,0:T(4,128)(2,1)} %bitcast.72) | data formatting | bytes 524288
  85.6 10.6 %all_to_all.53 = bf16[16,2,4096]{2,1,0:T(2,128)(2,1)S(1)} all-to-all(bf16[16,2,4096]{2,1,0:T(2,128)(2,1)S(1)} %reshape.97), channel_id=1, replica_groups=mesh['sp'=16,'tp'=4,'dp'=4] {'sp'}, dimensions={0} | all-to-all | bytes 524288 | tf_op jit(solution)/shard_map/all_to_all | solution.py:89
  96.2 5.9 %reshape.98 = bf16[4096,1,4,8]{3,2,1,0:T(4,128)(2,1)} reshape(bf16[16,2,4096]{2,1,0:T(2,128)(2,1)S(1)} %all_to_all.53) | data formatting | bytes 524288
  102.1 5.5 %copy.65 = bf16[4,1,8,16,256]{4,2,3,0,1:T(8,128)(2,1)S(1)} copy(bf16[4,1,8,16,256]{2,0,4,3,1:T(4,128)(2,1)} %bitcast.69) | data formatting | bytes 524288 | tf_op jit(solution)/shard_map/all_to_all | solution.py:89
  113.7 1.6 fusion.2
  115.4 1.8 fusion.31
  117.6 22.3 %all-gather.6.cloned.1.call-done = bf16[256,5120]{1,0:T(8,128)(2,1)} async-done(((bf16[256,1280]{1,0:T(8,128)(2,1)}), bf16[256,5120]{1,0:T(8,128)(2,1)}) %all-gather.6.cloned.1.call-update) | async-done | bytes 2621456 | tf_op jit(solution)/shard_map/all_gather | solution.py:110
  139.9 5.6 %convolution_convert_fusion = bf16[4,16,8,5120]{3,2,1,0:T(8,128)(2,1)} fusion(bf16[4,16,8,256]{3,2,1,0:T(8,128)(2,1)S(1)} %dot_general.24, bf16[256,5120]{1,0:T(8,128)(2,1)} %all-gather.6.cloned.1.call-done), kind=kOutput, calls=%fused_computation.4 | convolution fusion | flops 1344798720 | bytes 8126464 | tf_op jit(solution)/shard_map/dot_general | solution.py:108
  146.8 137.3 %all-reduce.5.cloned.1.call-done = bf16[4,16,8,5120]{3,2,1,0:T(8,128)(2,1)} async-done(((bf16[4,16,8,5120]{3,2,1,0:T(8,128)(2,1)}), bf16[4,16,8,5120]{3,2,1,0:T(8,128)(2,1)}) %all-reduce.5.cloned.1.call-update) | async-done | bytes 5242896
  284.1 1.8 convert_reduce_fusion
  286.7 5.1 %collective-permute-start.1 = (bf16[4,1,16,16]{3,2,1,0:T(8,128)(2,1)S(1)}, bf16[4,1,16,16]{3,2,1,0:T(8,128)(2,1)S(1)}, u32[]{:S(2)}, u32[]{:S(2)}) collective-permute-start(bf16[4,1,16,16]{3,2,1,0:T(8,128)(2,1)S(1)} %get-tuple-element.56), channel_id=1, source_target_pairs={{16,0},{32,16},{48,32},{64,48},{80,64},{96,80},{112,96},{128,112},... | collective-permute-start | bytes 6152 | tf_op jit(solution)/shard_map/ppermute | solution.py:17
  291.9 1.9 collective-permute-start
  293.8 5.2 %collective-permute-done = bf16[4,1,16,16]{3,2,1,0:T(8,128)(2,1)S(1)} collective-permute-done((bf16[4,1,16,16]{3,2,1,0:T(8,128)(2,1)S(1)}, bf16[4,1,16,16]{3,2,1,0:T(8,128)(2,1)S(1)}, u32[]{:S(2)}, u32[]{:S(2)}) %collective-permute-start) | collective-permute-done | bytes 2080 | tf_op jit(solution)/shard_map/ppermute | solution.py:14
  299.1 2.8 collective-permute-start.3
  303.2 4.2 %collective-permute-done.2 = bf16[4,4,1,16]{3,2,1,0:T(2,128)(2,1)S(1)} collective-permute-done((bf16[4,4,1,16]{3,2,1,0:T(2,128)(2,1)S(1)}, bf16[4,4,1,16]{3,2,1,0:T(2,128)(2,1)S(1)}, u32[]{:S(2)}, u32[]{:S(2)}) %collective-permute-start.2) | collective-permute-done | bytes 544 | tf_op jit(solution)/shard_map/ppermute | solution.py:14
  308.5 1.9 collective-permute-start.5
  310.5 2.4 collective-permute-start.4
  312.9 5.1 %collective-permute-done.4 = bf16[4,1,16,384]{3,2,1,0:T(8,128)(2,1)S(1)} collective-permute-done((bf16[4,1,16,384]{3,2,1,0:T(8,128)(2,1)S(1)}, bf16[4,1,16,384]{3,2,1,0:T(8,128)(2,1)S(1)}, u32[]{:S(2)}, u32[]{:S(2)}) %collective-permute-start.4) | collective-permute-done | bytes 49184 | tf_op jit(solution)/shard_map/ppermute | solution.py:14
  318.0 2.5 collective-permute-start.7
  322.0 4.2 %collective-permute-done.6 = bf16[4,4,1,384]{3,2,1,0:T(2,128)(2,1)S(1)} collective-permute-done((bf16[4,4,1,384]{3,2,1,0:T(2,128)(2,1)S(1)}, bf16[4,4,1,384]{3,2,1,0:T(2,128)(2,1)S(1)}, u32[]{:S(2)}, u32[]{:S(2)}) %collective-permute-start.6) | collective-permute-done | bytes 12320 | tf_op jit(solution)/shard_map/ppermute | solution.py:14
  327.6 5.5 %fusion.18 = bf16[4,2,16,384]{3,2,1,0:T(8,128)(2,1)} fusion(f32[4,2,16,384]{3,2,1,0:T(8,128)S(1)} %get-tuple-element.60, bf16[4,2,16,10368]{3,2,1,0:T(8,128)(2,1)S(1)} %slice_dynamic-update-slice_fusion, bf16[10368,384]{1,0:T(8,128)(2,1)} %param.26, f32[384]{0:T(512)S(1)} %copy-done.11), kind=kOutput, calls=%fused_computation.15 | convolution fusion | flops 1019363328 | bytes 10913280 | tf_op jit(solution)/shard_map/dot_general | solution.py:56
  (102 shorter events, 14.6 us)
Async XLA Ops:
  7.2 279.0 %copy-start = (bf16[5120,64]{0,1:T(8,128)(2,1)S(1)}, bf16[5120,64]{0,1:T(8,128)(2,1)}, u32[]{:S(2)}) copy-start(bf16[5120,64]{0,1:T(8,128)(2,1)} %param.22) | copy-start | bytes 1966084
  7.2 100.5 %all-gather.10.cloned.1.call-start = ((), (), s32[]{:S(2)}) async-start(), calls=%async_computation.5 | async-start | bytes 1310720 | tf_op jit(solution)/shard_map/all_gather | solution.py:95
  37.1 5.3 %copy-start.5 = (bf16[4,1,8,4096]{3,2,1,0:T(8,128)(2,1)S(1)}, bf16[4,1,8,4096]{3,2,1,0:T(8,128)(2,1)}, u32[]{:S(2)}) copy-start(bf16[4,1,8,4096]{3,2,1,0:T(8,128)(2,1)} %param.15) | copy-start | bytes 786436
  42.3 68.2 %all-gather.8.cloned.1.call-start = ((), (), s32[]{:S(2)}) async-start(), calls=%async_computation.4 | async-start | bytes 1310720 | tf_op jit(solution)/shard_map/all_gather | solution.py:94
  69.2 6.0 %copy-start.6 = (bf16[4,1,8,4096]{3,2,1,0:T(8,128)(2,1)S(1)}, bf16[4,1,8,4096]{3,2,1,0:T(8,128)(2,1)}, u32[]{:S(2)}) copy-start(bf16[4,1,8,4096]{3,2,1,0:T(8,128)(2,1)} %param.14) | copy-start | bytes 786436
  74.4 65.5 %all-gather.6.cloned.1.call-start = ((), (), s32[]{:S(2)}) async-start(), calls=%async_computation.3 | async-start | bytes 3276800 | tf_op jit(solution)/shard_map/all_gather | solution.py:110
  75.2 208.9 %all-reduce.5.cloned.1.call-start = ((), (), s32[]{:S(2)}) async-start(), calls=%async_computation.6 | async-start | bytes 10485760
  113.7 1.7 copy-start.2
  145.5 0.7 copy-start.13
  145.5 1.3 copy-start.7
  145.5 138.6 %copy-start.4 = (bf16[4,1,8,5120]{3,2,1,0:T(8,128)(2,1)S(1)}, bf16[4,1,8,5120]{3,2,1,0:T(8,128)(2,1)}, u32[]{:S(2)}) copy-start(bf16[4,1,8,5120]{3,2,1,0:T(8,128)(2,1)} %param.17) | copy-start | bytes 983044
  145.5 138.6 %copy-start.8 = (f32[5120]{0:T(1024)S(1)}, f32[5120]{0:T(1024)}, u32[]{:S(2)}) copy-start(f32[5120]{0:T(1024)} %param.19) | copy-start | bytes 61444
  145.5 140.7 %copy-start.12 = (f32[5120]{0:T(1024)S(1)}, f32[5120]{0:T(1024)}, u32[]{:S(2)}) copy-start(f32[5120]{0:T(1024)} %param.20) | copy-start | bytes 61444
  285.9 22.4 %copy-start.1 = (bf16[4,1,8,5120]{3,2,1,0:T(8,128)(2,1)}, bf16[4,1,8,5120]{3,2,1,0:T(8,128)(2,1)S(1)}, u32[]{:S(2)}) copy-start(bf16[4,1,8,5120]{3,2,1,0:T(8,128)(2,1)S(1)} %get-tuple-element.13) | copy-start | bytes 983044
  285.9 22.1 %copy-start.3 = (bf16[432,384]{1,0:T(8,128)(2,1)S(1)}, bf16[432,384]{1,0:T(8,128)(2,1)}, u32[]{:S(2)}) copy-start(bf16[432,384]{1,0:T(8,128)(2,1)} %param.23) | copy-start | bytes 995332
  285.9 22.1 %copy-start.10 = (f32[384]{0:T(512)S(1)}, f32[384]{0:T(512)}, u32[]{:S(2)}) copy-start(f32[384]{0:T(512)} %param.24) | copy-start | bytes 4612
  286.2 22.1 %copy-start.9 = (f32[384]{0:T(512)S(1)}, f32[384]{0:T(512)}, u32[]{:S(2)}) copy-start(f32[384]{0:T(512)} %param.25) | copy-start | bytes 4612
  286.7 7.1 %collective-permute-start.1 = (bf16[4,1,16,16]{3,2,1,0:T(8,128)(2,1)S(1)}, bf16[4,1,16,16]{3,2,1,0:T(8,128)(2,1)S(1)}, u32[]{:S(2)}, u32[]{:S(2)}) collective-permute-start(bf16[4,1,16,16]{3,2,1,0:T(8,128)(2,1)S(1)} %get-tuple-element.56), channel_id=1, source_target_pairs={{16,0},{32,16},{48,32},{64,48},{80,64},{96,80},{112,96},{128,112},... | collective-permute-start | bytes 6152 | tf_op jit(solution)/shard_map/ppermute | solution.py:17
  291.9 7.2 %collective-permute-start = (bf16[4,1,16,16]{3,2,1,0:T(8,128)(2,1)S(1)}, bf16[4,1,16,16]{3,2,1,0:T(8,128)(2,1)S(1)}, u32[]{:S(2)}, u32[]{:S(2)}) collective-permute-start(bf16[4,1,16,16]{3,2,1,0:T(8,128)(2,1)S(1)} %get-tuple-element.55), channel_id=1, source_target_pairs={{0,16},{16,32},{32,48},{48,64},{64,80},{80,96},{96,112},{112,128},... | collective-permute-start | bytes 6152 | tf_op jit(solution)/shard_map/ppermute | solution.py:14
  299.1 4.1 %collective-permute-start.3 = (bf16[4,4,1,16]{3,2,1,0:T(2,128)(2,1)S(1)}, bf16[4,4,1,16]{3,2,1,0:T(2,128)(2,1)S(1)}, u32[]{:S(2)}, u32[]{:S(2)}) collective-permute-start(bf16[4,4,1,16]{3,2,1,0:T(2,128)(2,1)S(1)} %get-tuple-element.52), channel_id=1, source_target_pairs={{4,0},{8,4},{12,8},{5,1},{9,5},{13,9},{6,2},{10,6},{14,10},{7,3},{... | collective-permute-start | bytes 1544 | tf_op jit(solution)/shard_map/ppermute | solution.py:17
  301.8 5.5 %collective-permute-start.2 = (bf16[4,4,1,16]{3,2,1,0:T(2,128)(2,1)S(1)}, bf16[4,4,1,16]{3,2,1,0:T(2,128)(2,1)S(1)}, u32[]{:S(2)}, u32[]{:S(2)}) collective-permute-start(bf16[4,4,1,16]{3,2,1,0:T(2,128)(2,1)S(1)} %get-tuple-element.51), channel_id=1, source_target_pairs={{0,4},{4,8},{8,12},{1,5},{5,9},{9,13},{2,6},{6,10},{10,14},{3,7},{... | collective-permute-start | bytes 1544 | tf_op jit(solution)/shard_map/ppermute | solution.py:14
  308.5 4.3 %collective-permute-start.5 = (bf16[4,1,16,384]{3,2,1,0:T(8,128)(2,1)S(1)}, bf16[4,1,16,384]{3,2,1,0:T(8,128)(2,1)S(1)}, u32[]{:S(2)}, u32[]{:S(2)}) collective-permute-start(bf16[4,1,16,384]{3,2,1,0:T(8,128)(2,1)S(1)} %get-tuple-element.42), channel_id=1, source_target_pairs={{16,0},{32,16},{48,32},{64,48},{80,64},{96,80},{112,96},{128,112},... | collective-permute-start | bytes 147464 | tf_op jit(solution)/shard_map/ppermute | solution.py:17
  310.5 7.5 %collective-permute-start.4 = (bf16[4,1,16,384]{3,2,1,0:T(8,128)(2,1)S(1)}, bf16[4,1,16,384]{3,2,1,0:T(8,128)(2,1)S(1)}, u32[]{:S(2)}, u32[]{:S(2)}) collective-permute-start(bf16[4,1,16,384]{3,2,1,0:T(8,128)(2,1)S(1)} %get-tuple-element.41), channel_id=1, source_target_pairs={{0,16},{16,32},{32,48},{48,64},{64,80},{80,96},{96,112},{112,128},... | collective-permute-start | bytes 147464 | tf_op jit(solution)/shard_map/ppermute | solution.py:14
  318.0 4.0 %collective-permute-start.7 = (bf16[4,4,1,384]{3,2,1,0:T(2,128)(2,1)S(1)}, bf16[4,4,1,384]{3,2,1,0:T(2,128)(2,1)S(1)}, u32[]{:S(2)}, u32[]{:S(2)}) collective-permute-start(bf16[4,4,1,384]{3,2,1,0:T(2,128)(2,1)S(1)} %get-tuple-element.22), channel_id=1, source_target_pairs={{4,0},{8,4},{12,8},{5,1},{9,5},{13,9},{6,2},{10,6},{14,10},{7,3},{... | collective-permute-start | bytes 36872 | tf_op jit(solution)/shard_map/ppermute | solution.py:17
  320.5 5.7 %collective-permute-start.6 = (bf16[4,4,1,384]{3,2,1,0:T(2,128)(2,1)S(1)}, bf16[4,4,1,384]{3,2,1,0:T(2,128)(2,1)S(1)}, u32[]{:S(2)}, u32[]{:S(2)}) collective-permute-start(bf16[4,4,1,384]{3,2,1,0:T(2,128)(2,1)S(1)} %get-tuple-element.21), channel_id=1, source_target_pairs={{0,4},{4,8},{8,12},{1,5},{5,9},{9,13},{2,6},{6,10},{10,14},{3,7},{... | collective-permute-start | bytes 36872 | tf_op jit(solution)/shard_map/ppermute | solution.py:14
  326.5 1.1 copy-start.11
Sparse Core Ops, SparseCore 0:
  42.4 25.9 all-gather.9
  74.5 26.2 all-gather.7
  102.7 37.2 all-gather.5
  145.7 138.3 all-reduce.4
where the time goes:
time: 341 us; the launch traced here: 340 us
  waiting for transfers between devices  179 us (52%)
  local copies, waits for them, and re-layouts  73.5 us (22%)
  blocking collectives  33.8 us (10%)
  starting transfers between devices  19.6 us (6%)
  matrix products  15 us (4%)
  between operations  14.3 us (4%)
  other arithmetic  4.54 us (1%)
    unnamed x5, waiting for transfers between devices  138 us
    unnamed x61, local copies, waits for them, and re-layouts  51.9 us
    all_gather x1, waiting for transfers between devices, shards(): lax.all_gather(out_weight, 'tp', axis=1, tiled=True)  22.3 us
    ppermute x4, waiting for transfers between devices, padded_2(): lax.ppermute(lax.slice_in_dim(block, block.shape[dim] - width, None, axis...  18.7 us
    all_to_all x1, blocking collectives, shards(): lax.all_to_all(values, 'sp', split_axis=3, concat_axis=1, tiled=True)  12.5 us
    ppermute x4, starting transfers between devices, padded_2(): lax.ppermute(lax.slice_in_dim(block, 0, width, axis=dim), axis, backward)  12.3 us
    all_to_all x1, blocking collectives, shards(): lax.all_to_all(queries, 'sp', split_axis=3, concat_axis=1, tiled=True)  10.6 us
    all_to_all x1, blocking collectives, shards(): lax.all_to_all(key_proj, 'sp', split_axis=3, concat_axis=1, tiled=True)  10.6 us
  transfers between devices with their start and end apart: 12, of which 6 were waited for; matrix products, arithmetic and copies ran while one was open for 16% of the time, Pallas kernels for 0%

commit v1 on v0

v1 whole, which is shorter than its diff:
```python
import jax
import jax.numpy as jnp
from jax import lax
from jax.experimental import pallas as pl
from jax.experimental.pallas import tpu as pltpu
from jax.sharding import Mesh, PartitionSpec as P

HEAD_DIM = 128
BF16 = jnp.bfloat16
F32 = jnp.float32
VMEM = pl.BlockSpec(memory_space=pltpu.VMEM)
HBM = pl.BlockSpec(memory_space=pltpu.HBM)


def in_hbm(array):
    return pltpu.with_memory_space_constraint(array, pltpu.HBM)


def call(kernel, out_shape, args, limit, bytes_accessed):
    return pl.pallas_call(
        kernel,
        out_shape=out_shape,
        in_specs=[VMEM] * len(args),
        out_specs=jax.tree.map(lambda _: VMEM, out_shape),
        compiler_params=pltpu.CompilerParams(vmem_limit_bytes=limit * 1024 * 1024),
        cost_estimate=pl.CostEstimate(flops=0, bytes_accessed=bytes_accessed, transcendentals=0),
    )(*args)


def pack_kernel(q_ref, k_ref, v_ref, w_ref, out_ref, low_ref, high_ref, inner_ref, held, packed, sems, out_sems):
    heads = out_ref.shape[0]
    step = w_ref.shape[0] // (sems.shape[0] - 3)
    copies = [
        pltpu.make_async_copy(ref, held.at[at], sems.at[at]) for at, ref in enumerate((q_ref, k_ref, v_ref))
    ]
    taken = 0
    for ref in (low_ref, high_ref, inner_ref):
        for row in range(0, ref.shape[0], step):
            source = w_ref.at[taken + row : taken + row + step]
            copies.append(pltpu.make_async_copy(source, ref.at[row : row + step], sems.at[len(copies)]))
        taken += ref.shape[0]
    for copy in copies:
        copy.start()
    sends = []
    for at in range(3):
        copies[at].wait()
        for h in range(heads):
            packed[at, h] = held[at, :, h * HEAD_DIM : (h + 1) * HEAD_DIM]
        place = out_ref.at[:, :, at * HEAD_DIM : (at + 1) * HEAD_DIM]
        sends.append(pltpu.make_async_copy(packed.at[at], place, out_sems.at[at]))
        sends[at].start()
    for copy in copies[3:] + sends:
        copy.wait()


FACTOR = HEAD_DIM ** (-0.5) * 1.4426950408889634


def scores_of(queries_ref, keys_ref, at):
    q = jnp.concatenate([queries_ref[2 * at + i, :, 0:HEAD_DIM] for i in range(2)], axis=0)
    k = keys_ref[:, :, HEAD_DIM : 2 * HEAD_DIM].reshape(-1, HEAD_DIM)
    return lax.dot_general(q, k, (((1,), (1,)), ((), ())), preferred_element_type=F32)


def own_attention_kernel(own_ref, mixed_ref, top_ref, total_ref):
    blocks = mixed_ref.shape[0]
    values = own_ref[:, :, 2 * HEAD_DIM : 3 * HEAD_DIM].reshape(-1, HEAD_DIM)
    following = scores_of(own_ref, own_ref, 0)
    for at in range(blocks):
        scores = following
        if at + 1 < blocks:
            following = scores_of(own_ref, own_ref, at + 1)
        top = jnp.max(scores, axis=1, keepdims=True)
        expo = jnp.exp2((scores - top) * FACTOR)
        top_ref[at] = top
        total_ref[at] = jnp.sum(expo, axis=1, keepdims=True)
        mixed_ref[at] = jnp.dot(expo.astype(BF16), values, preferred_element_type=F32)


def attention_kernel(own_ref, other_ref, mixed_ref, top_ref, total_ref, out_ref, result, sems):
    blocks, block, _ = mixed_ref.shape
    n_zl, copies, count, _ = out_ref.shape
    values = other_ref[:, :, 2 * HEAD_DIM : 3 * HEAD_DIM].reshape(-1, HEAD_DIM)
    sends = []
    following = scores_of(own_ref, other_ref, 0)
    for at in range(blocks):
        scores = following
        if at + 1 < blocks:
            following = scores_of(own_ref, other_ref, at + 1)
        top = jnp.maximum(top_ref[at], jnp.max(scores, axis=1, keepdims=True))
        expo = jnp.exp2((scores - top) * FACTOR)
        held = jnp.exp2((top_ref[at] - top) * FACTOR)
        total = total_ref[at] * held + jnp.sum(expo, axis=1, keepdims=True)
        mixed = mixed_ref[at] * held + jnp.dot(expo.astype(BF16), values, preferred_element_type=F32)
        result[at] = (mixed / total).astype(BF16)
        zl, start = at * block // count, at * block % count
        for copy in range(copies):
            place = out_ref.at[zl, copy, start : start + block]
            sends.append(pltpu.make_async_copy(result.at[at], place, sems.at[at, copy]))
            sends[-1].start()
    for send in sends:
        send.wait()


def projection_kernel(att_ref, *refs):
    refs, (out_ref, held, total, sems) = refs[:-4], refs[-4:]
    targets, rows, cols = out_ref.shape
    steps, depth, _ = held.shape
    n_x = att_ref.shape[0] // steps
    zl, core = lax.axis_index("zl"), lax.axis_index("core")
    starts = (0, refs[1].shape[0], refs[1].shape[0] + refs[2].shape[0])
    layout = ((0, 0), (1, starts[0]), (1, starts[1]), (1, starts[2]))
    copies = [[] for _ in range(steps)]
    for at, ref in enumerate(refs):
        step, start = layout[at % len(layout)]
        offset = (core if at < len(layout) else 1 - core) * (depth // 2)
        place = pl.ds(pl.multiple_of(offset + start, 16), ref.shape[0])
        copies[step].append(pltpu.make_async_copy(ref, held.at[step, place], sems.at[at]))
    for step in range(steps):
        for copy in copies[step]:
            copy.start()
    for step in range(steps):
        base = (zl if step == 0 else 1 - zl) * n_x
        feats = jnp.concatenate([att_ref[base + x] for x in range(n_x)], axis=1)
        for copy in copies[step]:
            copy.wait()
        term = jnp.dot(feats, held[step], preferred_element_type=F32)
        if step == 0:
            total[...] = term
        else:
            out_ref[...] = (total[...] + term).astype(BF16).reshape(targets, rows, cols)


def fetch_kernel(skip, after_ref, weight_ref, out_ref, sems):
    pieces = sems.shape[0]
    step = out_ref.shape[0] // pieces
    copies = [
        pltpu.make_async_copy(
            weight_ref.at[skip + at * step : skip + (at + 1) * step],
            out_ref.at[at * step : (at + 1) * step],
            sems.at[at],
        )
        for at in range(pieces)
    ]
    for copy in copies:
        copy.start()
    for copy in copies:
        copy.wait()


def fetch(weight, skip, rows, after):
    fetched = pl.pallas_call(
        lambda *refs: fetch_kernel(skip, *refs),
        out_shape=pltpu.VMEM((rows, weight.shape[1]), BF16),
        in_specs=[pl.BlockSpec(memory_space=pl.ANY), HBM],
        out_specs=VMEM,
        scratch_shapes=[pltpu.SemaphoreType.DMA((8,))],
        compiler_params=pltpu.CompilerParams(vmem_limit_bytes=8 * 1024 * 1024),
        cost_estimate=pl.CostEstimate(flops=0, bytes_accessed=4 * rows * weight.shape[1], transcendentals=0),
    )(after, in_hbm(weight))
    return pltpu.with_memory_space_constraint(fetched, pltpu.VMEM)


def head_kernel(splits, parts_ref, hidden_ref, gate_ref, shift_ref, scale_ref, head_ref, out_ref, patch_ref):
    quarters = parts_ref.shape[0] // splits
    tokens, cols = parts_ref.shape[1:]
    width = quarters * cols
    total = jnp.zeros((tokens, 1), F32)
    for quarter in range(quarters):
        span = slice(quarter * cols, (quarter + 1) * cols)
        acc = parts_ref[quarter].astype(F32)
        for split in range(1, splits):
            acc = acc + parts_ref[split * quarters + quarter].astype(F32)
        block_out = (hidden_ref[:, span].astype(F32) + gate_ref[:, span] * acc).astype(BF16)
        out_ref[:, span] = block_out
        total = total + jnp.sum(block_out.astype(F32), axis=1, keepdims=True)
    mean = total / width
    square = jnp.zeros((tokens, 1), F32)
    for quarter in range(quarters):
        span = slice(quarter * cols, (quarter + 1) * cols)
        centred = out_ref[:, span].astype(F32) - mean
        square = square + jnp.sum(centred * centred, axis=1, keepdims=True)
    inv = lax.rsqrt(square / width + 1e-06)
    patch = jnp.zeros((tokens, head_ref.shape[0]), F32)
    for quarter in range(quarters):
        span = slice(quarter * cols, (quarter + 1) * cols)
        centred = out_ref[:, span].astype(F32) - mean
        modded = (centred * inv * (1.0 + scale_ref[:, span]) + shift_ref[:, span]).astype(BF16)
        patch = patch + lax.dot_general(
            modded, head_ref[:, span], (((1,), (1,)), ((), ())), preferred_element_type=F32
        )
    patch_ref[...] = patch.astype(BF16).astype(F32)


def join_kernel(own_ref, left_ref, right_ref, after_ref, out_ref):
    col_at = lax.axis_index("tp")
    left = jnp.where(col_at == 0, 0.0, left_ref[...])
    right = jnp.where(col_at == 3, 0.0, right_ref[...])
    for f in range(out_ref.shape[0]):
        span = slice(8 * f, 8 * f + 8)
        out_ref[f, 0:8] = left[span]
        out_ref[f, 8:16] = own_ref[span]
        out_ref[f, 16:24] = right[span]


def decode_kernel(
    *refs,
):
    rows_in, refs = refs[:3], refs[3:]
    first_ref, bias1_ref, gain_ref, low_ref, high_ref, bias2_ref, out_ref, *refs = refs
    near, taps1, lhs1, first, active, lhs2, result = refs
    frames, cols = 4, 8
    lat = rows_in[0].shape[2] // 4
    chans = bias1_ref.shape[1]
    part = low_ref.shape[0]
    depth = (part + high_ref.shape[0]) // 3

    row_at = lax.axis_index(("zl", "y", "core"))
    col_at = lax.axis_index("tp")
    row_last, col_last = 15, 3
    near[...] = jnp.zeros_like(near)
    for r in range(3):
        row_out = (row_at == 0) if r == 0 else (row_at == row_last) if r == 2 else False
        rows = jnp.where(row_out, 0.0, rows_in[r][...])
        for f in range(frames):
            window = [rows[f, 7:15], rows[f, 8:16], rows[f, 9:17]]
            for a in range(2):
                span = slice(2 * lat * a, 2 * lat * (a + 1))
                row = jnp.concatenate(
                    [piece[:, span] for piece in window] + [jnp.zeros((cols, 128 - 6 * lat), F32)], axis=1
                )
                near[0, 2 + f, 2 * r + a] = row
                for v in range(1, 4):
                    near[v, 2 + f, 2 * r + a] = pltpu.roll(row, 128 - lat * v, 1)
    taps1[...] = jnp.zeros_like(taps1)
    for ti in range(9):
        taps1[128 * ti : 128 * ti + 3 * lat] = first_ref[3 * lat * ti : 3 * lat * (ti + 1)]
        t, i = ti // 3, ti % 3
        for v in range(4):
            piece = near[v, t : t + 4, i : i + 4].reshape(128, 128)
            lhs1[128 * v : 128 * (v + 1), 128 * ti : 128 * (ti + 1)] = piece.astype(BF16)

    col = lax.broadcasted_iota(jnp.int32, (frames, 4, cols, chans), 2)
    y = lax.broadcasted_iota(jnp.int32, (frames, 4, cols, chans), 1)
    outside_rows = ((y == 0) & (row_at == 0)) | ((y == 3) & (row_at == row_last))
    for v in range(4):
        value = jnp.dot(lhs1[128 * v : 128 * (v + 1)], taps1[...], preferred_element_type=F32) + bias1_ref[...]
        value = value.astype(BF16).astype(F32)
        if v in (1, 2):
            first[v - 1] = value.reshape(frames, 4, cols, chans)
        mean = jnp.mean(value * value, axis=1, keepdims=True)
        normed = value * lax.rsqrt(mean + 1e-06) * gain_ref[...]
        silu = (normed / (1.0 + jnp.exp(-normed))).reshape(frames, 4, cols, chans)
        outside = outside_rows
        if v == 0:
            outside = outside | ((col == 0) & (col_at == 0))
        if v == 3:
            outside = outside | ((col == cols - 1) & (col_at == col_last))
        active[:, :, v] = jnp.where(outside, 0.0, silu)

    for i in range(3):
        for j in range(3):
            piece = active[:, i : i + 2, j : j + 2].reshape(128, chans)
            at = chans * (3 * i + j)
            lhs2[:, at : at + chans] = piece.astype(BF16)
    total = jnp.zeros((128, chans), F32)
    for t in (2, 1, 0):
        rows = 32 * (2 + t)
        start, stop = depth * t, depth * (t + 1)
        term = jnp.zeros((rows, chans), F32)
        for ref, first_row in ((low_ref, 0), (high_ref, part)):
            low, high = max(start, first_row), min(stop, first_row + ref.shape[0])
            if low < high:
                weight = ref[low - first_row : high - first_row]
                term += jnp.dot(lhs2[0:rows, low - start : high - start], weight, preferred_element_type=F32)
        if t < 2:
            term = jnp.concatenate([jnp.zeros((128 - rows, chans), F32), term], axis=0)
        total = total + term
    total = (total + bias2_ref[...]).reshape(frames, 2, 2, cols, chans)
    for f in range(frames):
        for a in range(2):
            for b in range(2):
                cell = total[f, a, b] + first[b, f, 1 + a]
                for n in range(chans // 128):
                    result[n, f, a, pl.ds(b, cols, stride=2)] = cell[:, 128 * n : 128 * (n + 1)]
    for n in range(chans // 128):
        out_ref[:, :, :, 128 * n : 128 * (n + 1)] = result[n].astype(BF16)


def neighbours(block, axis):
    count = lax.axis_size(axis)
    forward = [(i, (i + 1) % count) for i in range(count)]
    backward = [(target, source) for source, target in forward]
    return lax.ppermute(block, axis, forward), lax.ppermute(block, axis, backward)


def shards(
    queries,
    key_proj,
    values,
    hidden_in,
    out_weight,
    out_gate,
    mod_shift,
    mod_scale,
    head_weight,
    conv_first,
    bias_first,
    norm_gain,
    conv_second,
    bias_second,
):
    frames, row_dev, col_dev, features = queries.shape
    width = hidden_in.shape[3]
    tokens = frames * row_dev * col_dev
    heads = features // HEAD_DIM
    n_zl, n_y, n_x, n_dp = (lax.axis_size(a) for a in ("zl", "y", "tp", "dp"))
    chips = n_zl * n_y * n_x
    assert heads == chips

    depth, n_cols = out_weight.shape
    weight_parts = [jax.ShapeDtypeStruct((rows, n_cols), BF16) for rows in (depth * 3 // 8, depth // 2, depth // 8)]
    packed, weight_low, weight_high, weight_inner = pl.pallas_call(
        pack_kernel,
        out_shape=(jax.ShapeDtypeStruct((heads, tokens, 3 * HEAD_DIM), BF16), *weight_parts),
        in_specs=[HBM] * 4,
        out_specs=(HBM, HBM, HBM, HBM),
        scratch_shapes=[
            pltpu.VMEM((3, tokens, features), BF16),
            pltpu.VMEM((3, heads, tokens, HEAD_DIM), BF16),
            pltpu.SemaphoreType.DMA((3 + 16,)),
            pltpu.SemaphoreType.DMA((3,)),
        ],
        compiler_params=pltpu.CompilerParams(vmem_limit_bytes=24 * 1024 * 1024),
    )(*[in_hbm(a.reshape(tokens, features)) for a in (queries, key_proj, values)], in_hbm(out_weight))
    own = lax.all_to_all(packed, ("zl", "y", "tp"), 0, 0, tiled=True)
    swap = [(0, 1), (1, 0)]
    outer = []
    for dp in range(n_dp):
        low, high = dp, n_dp + (dp - 1) % n_dp
        outer += [(low, high), (high, low)]
    from_first = lax.ppermute(weight_high, ("zl", "dp"), outer)
    from_inner = lax.ppermute(weight_inner, "zl", swap)
    own, from_first, from_inner = lax.optimization_barrier((own, from_first, from_inner))
    other = lax.ppermute(own, "core", swap)
    sources = (n_zl * n_y, n_x * tokens, 3 * HEAD_DIM)
    held = n_y * n_x * tokens
    blocks, block = n_zl * held // 256, 256
    stat = jax.ShapeDtypeStruct((blocks, block, 1), F32)
    own, other = own.reshape(sources), other.reshape(sources)
    mixed, top, total = call(
        own_attention_kernel,
        (jax.ShapeDtypeStruct((blocks, block, HEAD_DIM), F32), stat, stat),
        [own],
        limit=24,
        bytes_accessed=8 * 1024 * 1024,
    )
    attended_here = pl.pallas_call(
        attention_kernel,
        out_shape=jax.ShapeDtypeStruct((n_zl, n_x, held, HEAD_DIM), BF16),
        in_specs=[VMEM] * 5,
        out_specs=HBM,
        scratch_shapes=[
            pltpu.VMEM((blocks, block, HEAD_DIM), BF16),
            pltpu.SemaphoreType.DMA((blocks, n_x)),
        ],
        compiler_params=pltpu.CompilerParams(vmem_limit_bytes=24 * 1024 * 1024),
    )(own, other, mixed, top, total)
    attended = lax.all_to_all(
        attended_here.reshape(n_zl * n_x, held, HEAD_DIM), ("zl", "tp"), 0, 0, tiled=True
    )
    weight_low, out_weight, from_first, from_inner, _ = lax.optimization_barrier(
        (weight_low, out_weight, from_first, from_inner, attended_here)
    )
    from_last = lax.ppermute(weight_low, ("zl", "dp"), outer)
    near = (out_weight, from_last, from_first, from_inner)
    far = tuple(lax.ppermute(piece, "core", swap) for piece in near)
    terms = pl.pallas_call(
        projection_kernel,
        out_shape=jax.ShapeDtypeStruct((n_y * n_x, tokens, n_cols), BF16),
        in_specs=[VMEM] + [HBM] * 5 + [VMEM, HBM, HBM],
        out_specs=VMEM,
        scratch_shapes=[
            pltpu.VMEM((n_zl, 2 * out_weight.shape[0], n_cols), BF16),
            pltpu.VMEM((held, n_cols), F32),
            pltpu.SemaphoreType.DMA((8,)),
        ],
        compiler_params=pltpu.CompilerParams(vmem_limit_bytes=24 * 1024 * 1024),
    )(
        attended,
        *[in_hbm(piece) for piece in near + far[:1]],
        pltpu.with_memory_space_constraint(far[1], pltpu.VMEM),
        *[in_hbm(piece) for piece in far[2:]],
    )
    terms = lax.all_to_all(terms, ("y", "tp"), 0, 0, tiled=True)
    patch_width = head_weight.shape[1]
    block_out, patch = call(
        lambda *refs: head_kernel(n_y, *refs),
        (
            jax.ShapeDtypeStruct((tokens, width), BF16),
            jax.ShapeDtypeStruct((tokens, patch_width), F32),
        ),
        [
            terms,
            hidden_in.reshape(tokens, width),
            out_gate.reshape(1, width),
            mod_shift.reshape(1, width),
            mod_scale.reshape(1, width),
            head_weight.T,
        ],
        limit=12,
        bytes_accessed=16 * 1024 * 1024,
    )
    block_out = block_out.reshape(hidden_in.shape)

    left, right = neighbours(patch, "tp")
    part = conv_second.shape[0] // 256 * 128
    second_low = fetch(conv_second, 0, part, patch)
    joined = call(
        join_kernel,
        jax.ShapeDtypeStruct((frames, 24, patch_width), F32),
        [patch, left, right, second_low],
        limit=4,
        bytes_accessed=8 * 1024 * 1024,
    )
    above, below = neighbours(joined, ("zl", "y", "core"))
    second_high = fetch(conv_second, part, conv_second.shape[0] - part, joined)
    chans = conv_first.shape[1]
    depth = conv_second.shape[0] // 3
    decoded = pl.pallas_call(
        decode_kernel,
        out_shape=jax.ShapeDtypeStruct((frames, 2 * row_dev, 2 * col_dev, chans), BF16),
        in_specs=[VMEM] * 9,
        out_specs=VMEM,
        scratch_shapes=[
            pltpu.VMEM((4, frames + 2, 6, col_dev, 128), F32),
            pltpu.VMEM((9 * 128, chans), BF16),
            pltpu.VMEM((4 * 128, 9 * 128), BF16),
            pltpu.VMEM((2, frames, 4, col_dev, chans), F32),
            pltpu.VMEM((frames, 4, 4, col_dev, chans), F32),
            pltpu.VMEM((128, depth), BF16),
            pltpu.VMEM((chans // 128, frames, 2, 2 * col_dev, 128), F32),
        ],
        compiler_params=pltpu.CompilerParams(vmem_limit_bytes=32 * 1024 * 1024),
    )(
        above,
        joined,
        below,
        conv_first,
        bias_first.reshape(1, chans),
        norm_gain.reshape(1, chans),
        second_low,
        second_high,
        bias_second.reshape(1, chans),
    )
    return (block_out, decoded)


def solution(mesh):
    fine = Mesh(mesh.devices.reshape(2, 4, 2, *mesh.devices.shape[1:]), ("zl", "y", "core", "tp", "dp"))
    sp = ("zl", "y", "core")
    grid = P("dp", sp, "tp", None)
    in_specs = (grid, grid, grid, grid, P(sp, "tp")) + (P(),) * 9
    return jax.shard_map(
        shards, mesh=fine, in_specs=in_specs, out_specs=(grid, grid), check_vma=False
    )
```

time: 341 us -> 94.6 us (0.28)
  the two profiles are of different devices: /device:TPU:38 before, /device:TPU:2 now
where the time goes in v1:
time: 94.6 us; the launch traced here: 94.2 us
  starting transfers between devices  27.8 us (29%)
  blocking collectives  25.1 us (27%)
  waiting for transfers between devices  20.5 us (22%)
  Pallas kernels  19 us (20%)
    all_to_all x1, blocking collectives, shards(): terms = lax.all_to_all(terms, ('y', 'tp'), 0, 0, tiled=True)  25.1 us
    all_to_all x1, starting transfers between devices, shards(): own = lax.all_to_all(packed, ('zl', 'y', 'tp'), 0, 0, tiled=True)  8.98 us
    ppermute x1, waiting for transfers between devices, shards(): from_last = lax.ppermute(weight_low, ('zl', 'dp'), outer)  6.38 us
    ppermute x1, waiting for transfers between devices, shards(): from_inner = lax.ppermute(weight_inner, 'zl', swap)  6.36 us
    ppermute x1, starting transfers between devices, shards(): from_first = lax.ppermute(weight_high, ('zl', 'dp'), outer)  5.5 us
    ppermute x1, starting transfers between devices, shards(): from_last = lax.ppermute(weight_low, ('zl', 'dp'), outer)  5.49 us
    all_to_all x1, starting transfers between devices, shards(): lax.all_to_all(attended_here.reshape(n_zl * n_x, held, HEAD_DIM), ('zl',...  4.52 us
    pallas_call x2, Pallas kernels, fetch(): pl.pallas_call(lambda *refs: fetch_kernel(skip, *refs), out_shape=pltpu.V...  4.34 us
  transfers between devices with their start and end apart: 14, of which 8 were waited for; matrix products, arithmetic and copies ran while one was open for 0% of the time, Pallas kernels for 6%

profile of v1, /device:TPU:2, one launch (start us, length us, event | category | flops | bytes accessed | tf_op | source)
XLA Modules:
  0.0 94.2 jit_solution(1394410678251599904)
XLA Ops:
  0.6 2.1 %shard_map.149 = (bf16[32,32,384]{2,1,0:T(8,128)(2,1)}, bf16[96,1280]{1,0:T(8,128)(2,1)S(1)}, bf16[128,1280]{1,0:T(8,128)(2,1)S(1)}, bf16[32,1280]{1,0:T(8,128)(2,1)S(1)}) custom-call(bf16[32,4096]{1,0:T(8,128)(2,1)} %bitcast.22, bf16[32,4096]{1,0:T(8,128)(2,1)} %bitcast.23, bf16[32,4096]{1,0:T(8,128)(2,1)} %bitcast.24, bf16[256,1280]{1,0:T(8,128)(2,1)} %refs_0_), custom_call_target="tpu_custom_call" | custom-call | tf_op jit(solution)/shard_map/pallas_call | solution.py:323
  2.7 9.0 %all-to-all-start = ((bf16[32,32,384]{2,1,0:T(8,128)(2,1)}), bf16[32,32,384]{2,1,0:T(8,128)(2,1)S(1)}, u32[]{:S(2)}, u32[]{:S(2)}) async-start(bf16[32,32,384]{2,1,0:T(8,128)(2,1)} %get-tuple-element.18), calls=%async_computation | async-start | bytes 1572864 | tf_op jit(solution)/shard_map/all_to_all | solution.py:336
  11.7 0.0 copy-start.6
  11.8 5.5 %collective-permute-start = (bf16[128,1280]{1,0:T(8,128)(2,1)S(1)}, bf16[128,1280]{1,0:T(8,128)(2,1)S(1)}, u32[]{:S(2)}, u32[]{:S(2)}) collective-permute-start(bf16[128,1280]{1,0:T(8,128)(2,1)S(1)} %get-tuple-element.19), channel_id=1, source_target_pairs={{0,131},{131,0},{1,128},{128,1},{2,129},{129,2},{3,130},{130,3},{4... | collective-permute-start | bytes 983048 | tf_op jit(solution)/shard_map/ppermute | solution.py:342
  17.2 6.4 %collective-permute-done.1.refs_3_ = bf16[32,1280]{1,0:T(8,128)(2,1)S(1)} collective-permute-done((bf16[32,1280]{1,0:T(8,128)(2,1)S(1)}, bf16[32,1280]{1,0:T(8,128)(2,1)S(1)}, u32[]{:S(2)}, u32[]{:S(2)}) %collective-permute-start.1) | collective-permute-done | bytes 81952 | tf_op jit(solution)/shard_map/ppermute | solution.py:343
  23.6 0.8 collective-permute-done.refs_2_
  24.4 1.2 %all-to-all-done = bf16[32,32,384]{2,1,0:T(8,128)(2,1)S(1)} async-done(((bf16[32,32,384]{2,1,0:T(8,128)(2,1)}), bf16[32,32,384]{2,1,0:T(8,128)(2,1)S(1)}, u32[]{:S(2)}, u32[]{:S(2)}) %all-to-all-start) | async-done | bytes 786464 | tf_op jit(solution)/shard_map/all_to_all | solution.py:336
  25.6 1.5 %shard_map.150 = (f32[4,256,128]{2,1,0:T(8,128)S(1)}, f32[4,256,1]{2,1,0:T(8,128)S(1)}, f32[4,256,1]{2,1,0:T(8,128)S(1)}) custom-call(bf16[8,128,384]{2,1,0:T(8,128)(2,1)S(1)} %bitcast.14), custom_call_target="tpu_custom_call" | custom-call | bytes 8388608 | tf_op jit(solution)/shard_map/pallas_call | solution.py:20
  27.0 0.8 collective-permute-done.2
  27.8 3.0 %shard_map.151 = bf16[2,4,512,128]{3,2,1,0:T(8,128)(2,1)} custom-call(bf16[8,128,384]{2,1,0:T(8,128)(2,1)S(1)} %bitcast.15, bf16[8,128,384]{2,1,0:T(8,128)(2,1)S(1)} %bitcast.16, f32[4,256,128]{2,1,0:T(8,128)S(1)} %get-tuple-element.22.mixed_ref, f32[4,256,1]{2,1,0:T(8,128)S(1)} %get-tuple-element.23.top_ref, f32[4,256,1]{2,1,0:T(8,128)S(1)} %get-tuple-element.24.total_ref), custom_call_target="tpu_custom_call" | custom-call | tf_op jit(solution)/shard_map/pallas_call | solution.py:358
  30.8 4.5 %all-to-all-start.1 = ((bf16[8,512,128]{2,1,0:T(8,128)(2,1)}), bf16[8,512,128]{2,1,0:T(8,128)(2,1)S(1)}, u32[]{:S(2)}, u32[]{:S(2)}) async-start(bf16[8,512,128]{2,1,0:T(8,128)(2,1)} %bitcast.5), calls=%async_computation.1 | async-start | bytes 2097152 | tf_op jit(solution)/shard_map/all_to_all | solution.py:369
  35.3 0.0 copy-start.4
  35.4 0.1 collective-permute-start.4
  35.5 5.5 %collective-permute-start.3 = (bf16[96,1280]{1,0:T(8,128)(2,1)S(1)}, bf16[96,1280]{1,0:T(8,128)(2,1)S(1)}, u32[]{:S(2)}, u32[]{:S(2)}) collective-permute-start(bf16[96,1280]{1,0:T(8,128)(2,1)S(1)} %get-tuple-element.29), channel_id=1, source_target_pairs={{0,131},{131,0},{1,128},{128,1},{2,129},{129,2},{3,130},{130,3},{4... | collective-permute-start | bytes 737288 | tf_op jit(solution)/shard_map/ppermute | solution.py:375
  41.0 0.1 collective-permute-start.6
  41.1 6.4 %collective-permute-done.3.refs_1_ = bf16[96,1280]{1,0:T(8,128)(2,1)S(1)} collective-permute-done((bf16[96,1280]{1,0:T(8,128)(2,1)S(1)}, bf16[96,1280]{1,0:T(8,128)(2,1)S(1)}, u32[]{:S(2)}, u32[]{:S(2)}) %collective-permute-start.3) | collective-permute-done | bytes 245792 | tf_op jit(solution)/shard_map/ppermute | solution.py:375
  47.5 0.5 collective-permute-start.7
  48.0 1.1 %collective-permute-done.7.refs_7_ = bf16[32,1280]{1,0:T(8,128)(2,1)S(1)} collective-permute-done((bf16[32,1280]{1,0:T(8,128)(2,1)S(1)}, bf16[32,1280]{1,0:T(8,128)(2,1)S(1)}, u32[]{:S(2)}, u32[]{:S(2)}) %collective-permute-start.7) | collective-permute-done | bytes 81952 | tf_op jit(solution)/shard_map/ppermute | solution.py:377
  49.1 0.7 copy-done.8
  49.9 3.2 %shard_map.152 = bf16[16,32,1280]{2,1,0:T(8,128)(2,1)S(1)} custom-call(bf16[8,512,128]{2,1,0:T(8,128)(2,1)S(1)} %all-to-all-done.1.att_ref, bf16[256,1280]{1,0:T(8,128)(2,1)} %refs_0_, bf16[96,1280]{1,0:T(8,128)(2,1)} %copy-done.9, bf16[128,1280]{1,0:T(8,128)(2,1)} %copy-done.7, bf16[32,1280]{1,0:T(8,128)(2,1)} %copy-done.10, ...), custom_call_target="tpu_custom_call" | custom-call | tf_op jit(solution)/shard_map/pallas_call | solution.py:378
  53.2 25.1 %all_to_all.15.refs_0_ = bf16[16,32,1280]{2,1,0:T(8,128)(2,1)S(1)} all-to-all(bf16[16,32,1280]{2,1,0:T(8,128)(2,1)S(1)} %shard_map.152), channel_id=1, replica_groups=mesh['zl'=2,'y'=4,'core'=2,'tp'=4,'dp'=4] {'y','tp'}, dimensions={0} | all-to-all | bytes 2621440 | tf_op jit(solution)/shard_map/all_to_all | solution.py:395
  78.3 1.4 %shard_map.153 = (bf16[32,5120]{1,0:T(8,128)(2,1)}, f32[32,64]{1,0:T(8,128)S(1)}) custom-call(bf16[16,32,1280]{2,1,0:T(8,128)(2,1)S(1)} %all_to_all.15.refs_0_, bf16[32,5120]{1,0:T(8,128)(2,1)S(1)} %bitcast.18, f32[1,5120]{1,0:T(1,128)S(1)} %bitcast.19, f32[1,5120]{1,0:T(1,128)S(1)} %bitcast.20, f32[1,5120]{1,0:T(1,128)S(1)} %bitcast.21, ...), custom_call_target="tpu_custom_call" | custom-call | bytes 16777216 | tf_op jit(solution)/shard_map/pallas_call | solution.py:20
  79.7 1.5 %collective-permute-start.9 = (f32[32,64]{1,0:T(8,128)S(1)}, f32[32,64]{1,0:T(8,128)S(1)}, u32[]{:S(2)}, u32[]{:S(2)}) collective-permute-start(f32[32,64]{1,0:T(8,128)S(1)} %get-tuple-element.33.refs_0_.own_ref), channel_id=1, source_target_pairs={{4,0},{8,4},{12,8},{0,12},{5,1},{9,5},{13,9},{1,13},{6,2},{10,6},{... | collective-permute-start | bytes 24584 | tf_op jit(solution)/shard_map/ppermute | solution.py:294
  81.2 0.6 collective-permute-start.8
  81.7 2.1 %shard_map.154.after_ref.refs_6_ = bf16[5120,384]{1,0:T(8,128)(2,1)S(1)} custom-call(f32[32,64]{1,0:T(8,128)S(1)} %get-tuple-element.33.refs_0_.own_ref, bf16[10368,384]{1,0:T(8,128)(2,1)} %refs_1_.3), custom_call_target="tpu_custom_call" | custom-call | bytes 7864320 | tf_op jit(solution)/shard_map/pallas_call | solution.py:152
  83.9 0.0 copy-start.12
  83.9 1.0 %collective-permute-done.8.left_ref = f32[32,64]{1,0:T(8,128)S(1)} collective-permute-done((f32[32,64]{1,0:T(8,128)S(1)}, f32[32,64]{1,0:T(8,128)S(1)}, u32[]{:S(2)}, u32[]{:S(2)}) %collective-permute-start.8) | collective-permute-done | bytes 8224 | tf_op jit(solution)/shard_map/ppermute | solution.py:294
  84.9 0.1 collective-permute-start.11
  85.0 0.5 collective-permute-start.10
  85.5 2.2 %shard_map.156.refs_7_ = bf16[5248,384]{1,0:T(8,128)(2,1)S(1)} custom-call(f32[4,24,64]{2,1,0:T(8,128)S(1)} %shard_map.155.refs_0_.refs_1_, bf16[10368,384]{1,0:T(8,128)(2,1)} %refs_1_.3), custom_call_target="tpu_custom_call" | custom-call | bytes 8060928 | tf_op jit(solution)/shard_map/pallas_call | solution.py:152
  87.8 2.9 %collective-permute-done.10.refs_0_ = f32[4,24,64]{2,1,0:T(8,128)S(1)} collective-permute-done((f32[4,24,64]{2,1,0:T(8,128)S(1)}, f32[4,24,64]{2,1,0:T(8,128)S(1)}, u32[]{:S(2)}, u32[]{:S(2)}) %collective-permute-start.10) | collective-permute-done | bytes 24608 | tf_op jit(solution)/shard_map/ppermute | solution.py:294
  90.7 3.5 %shard_map.157 = bf16[4,2,16,384]{3,2,1,0:T(8,128)(2,1)} custom-call(f32[4,24,64]{2,1,0:T(8,128)S(1)} %collective-permute-done.10.refs_0_, f32[4,24,64]{2,1,0:T(8,128)S(1)} %shard_map.155.refs_0_.refs_1_, f32[4,24,64]{2,1,0:T(8,128)S(1)} %collective-permute-done.11.refs_2_, bf16[432,384]{1,0:T(8,128)(2,1)S(1)} %copy-done.1, f32[1,384]{1,0:T(1,128)S(1)} %reshape.57.refs_4_, ...), custom_call_target="tpu_custom_call" | custom-call | tf_op jit(solution)/shard_map/pallas_call | solution.py:430
  (39 shorter events, 0.1 us)
Async XLA Ops:
  2.7 22.8 %all-to-all-start = ((bf16[32,32,384]{2,1,0:T(8,128)(2,1)}), bf16[32,32,384]{2,1,0:T(8,128)(2,1)S(1)}, u32[]{:S(2)}, u32[]{:S(2)}) async-start(bf16[32,32,384]{2,1,0:T(8,128)(2,1)} %get-tuple-element.18), calls=%async_computation | async-start | bytes 1572864 | tf_op jit(solution)/shard_map/all_to_all | solution.py:336
  11.7 23.6 %copy-start.6 = (bf16[256,1280]{1,0:T(8,128)(2,1)S(1)}, bf16[256,1280]{1,0:T(8,128)(2,1)}, u32[]{:S(2)}) copy-start(bf16[256,1280]{1,0:T(8,128)(2,1)} %refs_0_) | copy-start | bytes 1966084
  11.8 12.6 %collective-permute-start = (bf16[128,1280]{1,0:T(8,128)(2,1)S(1)}, bf16[128,1280]{1,0:T(8,128)(2,1)S(1)}, u32[]{:S(2)}, u32[]{:S(2)}) collective-permute-start(bf16[128,1280]{1,0:T(8,128)(2,1)S(1)} %get-tuple-element.19), channel_id=1, source_target_pairs={{0,131},{131,0},{1,128},{128,1},{2,129},{129,2},{3,130},{130,3},{4... | collective-permute-start | bytes 983048 | tf_op jit(solution)/shard_map/ppermute | solution.py:342
  17.2 6.4 %collective-permute-start.1 = (bf16[32,1280]{1,0:T(8,128)(2,1)S(1)}, bf16[32,1280]{1,0:T(8,128)(2,1)S(1)}, u32[]{:S(2)}, u32[]{:S(2)}) collective-permute-start(bf16[32,1280]{1,0:T(8,128)(2,1)S(1)} %get-tuple-element.20), channel_id=1, source_target_pairs={{0,128},{128,0},{1,129},{129,1},{2,130},{130,2},{3,131},{131,3},{4... | collective-permute-start | bytes 245768 | tf_op jit(solution)/shard_map/ppermute | solution.py:343
  23.6 26.3 %copy-start.10 = (bf16[32,1280]{1,0:T(8,128)(2,1)}, bf16[32,1280]{1,0:T(8,128)(2,1)S(1)}, u32[]{:S(2)}) copy-start(bf16[32,1280]{1,0:T(8,128)(2,1)S(1)} %collective-permute-done.1.refs_3_) | copy-start | bytes 245764
  24.4 25.5 %copy-start.7 = (bf16[128,1280]{1,0:T(8,128)(2,1)}, bf16[128,1280]{1,0:T(8,128)(2,1)S(1)}, u32[]{:S(2)}) copy-start(bf16[128,1280]{1,0:T(8,128)(2,1)S(1)} %collective-permute-done.refs_2_) | copy-start | bytes 983044
  25.6 2.3 %collective-permute-start.2 = (bf16[32,32,384]{2,1,0:T(8,128)(2,1)S(1)}, bf16[32,32,384]{2,1,0:T(8,128)(2,1)S(1)}, u32[]{:S(2)}, u32[]{:S(2)}) collective-permute-start(bf16[32,32,384]{2,1,0:T(8,128)(2,1)S(1)} %all-to-all-done), channel_id=1, source_target_pairs={{0,16},{16,0},{1,17},{17,1},{2,18},{18,2},{3,19},{19,3},{4,20},{20... | collective-permute-start | bytes 2359304 | tf_op jit(solution)/shard_map/ppermute | solution.py:345
  30.8 19.1 %all-to-all-start.1 = ((bf16[8,512,128]{2,1,0:T(8,128)(2,1)}), bf16[8,512,128]{2,1,0:T(8,128)(2,1)S(1)}, u32[]{:S(2)}, u32[]{:S(2)}) async-start(bf16[8,512,128]{2,1,0:T(8,128)(2,1)} %bitcast.5), calls=%async_computation.1 | async-start | bytes 2097152 | tf_op jit(solution)/shard_map/all_to_all | solution.py:369
  35.3 43.0 %copy-start = (bf16[5120,64]{0,1:T(8,128)(2,1)S(1)}, bf16[5120,64]{0,1:T(8,128)(2,1)}, u32[]{:S(2)}) copy-start(bf16[5120,64]{0,1:T(8,128)(2,1)} %param.22) | copy-start | bytes 1966084
  35.3 43.0 %copy-start.2 = (bf16[4,1,8,5120]{3,2,1,0:T(8,128)(2,1)S(1)}, bf16[4,1,8,5120]{3,2,1,0:T(8,128)(2,1)}, u32[]{:S(2)}) copy-start(bf16[4,1,8,5120]{3,2,1,0:T(8,128)(2,1)} %param.17) | copy-start | bytes 983044
  35.3 43.0 %copy-start.3 = (f32[5120]{0:T(1024)S(1)}, f32[5120]{0:T(1024)}, u32[]{:S(2)}) copy-start(f32[5120]{0:T(1024)} %param.19) | copy-start | bytes 61444
  35.3 43.0 %copy-start.4 = (f32[5120]{0:T(1024)S(1)}, f32[5120]{0:T(1024)}, u32[]{:S(2)}) copy-start(f32[5120]{0:T(1024)} %param.20) | copy-start | bytes 61444
  35.4 43.0 %copy-start.5 = (f32[5120]{0:T(1024)S(1)}, f32[5120]{0:T(1024)}, u32[]{:S(2)}) copy-start(f32[5120]{0:T(1024)} %param.21) | copy-start | bytes 61444
  35.4 14.5 %collective-permute-start.4 = (bf16[256,1280]{1,0:T(8,128)(2,1)S(1)}, bf16[256,1280]{1,0:T(8,128)(2,1)}, u32[]{:S(2)}, u32[]{:S(2)}) collective-permute-start(bf16[256,1280]{1,0:T(8,128)(2,1)S(1)} %copy-done.6), channel_id=1, source_target_pairs={{0,16},{16,0},{1,17},{17,1},{2,18},{18,2},{3,19},{19,3},{4,20},{20... | collective-permute-start | bytes 1966088 | tf_op jit(solution)/shard_map/ppermute | solution.py:377
  35.5 12.0 %collective-permute-start.3 = (bf16[96,1280]{1,0:T(8,128)(2,1)S(1)}, bf16[96,1280]{1,0:T(8,128)(2,1)S(1)}, u32[]{:S(2)}, u32[]{:S(2)}) collective-permute-start(bf16[96,1280]{1,0:T(8,128)(2,1)S(1)} %get-tuple-element.29), channel_id=1, source_target_pairs={{0,131},{131,0},{1,128},{128,1},{2,129},{129,2},{3,130},{130,3},{4... | collective-permute-start | bytes 737288 | tf_op jit(solution)/shard_map/ppermute | solution.py:375
  41.0 8.2 %collective-permute-start.6 = (bf16[128,1280]{1,0:T(8,128)(2,1)S(1)}, bf16[128,1280]{1,0:T(8,128)(2,1)S(1)}, u32[]{:S(2)}, u32[]{:S(2)}) collective-permute-start(bf16[128,1280]{1,0:T(8,128)(2,1)S(1)} %collective-permute-done.refs_2_), channel_id=1, source_target_pairs={{0,16},{16,0},{1,17},{17,1},{2,18},{18,2},{3,19},{19,3},{4,20},{20... | collective-permute-start | bytes 983048 | tf_op jit(solution)/shard_map/ppermute | solution.py:377
  47.5 1.6 %copy-start.9 = (bf16[96,1280]{1,0:T(8,128)(2,1)}, bf16[96,1280]{1,0:T(8,128)(2,1)S(1)}, u32[]{:S(2)}) copy-start(bf16[96,1280]{1,0:T(8,128)(2,1)S(1)} %collective-permute-done.3.refs_1_) | copy-start | bytes 737284
  47.5 1.6 %collective-permute-start.5 = (bf16[96,1280]{1,0:T(8,128)(2,1)S(1)}, bf16[96,1280]{1,0:T(8,128)(2,1)S(1)}, u32[]{:S(2)}, u32[]{:S(2)}) collective-permute-start(bf16[96,1280]{1,0:T(8,128)(2,1)S(1)} %collective-permute-done.3.refs_1_), channel_id=1, source_target_pairs={{0,16},{16,0},{1,17},{17,1},{2,18},{18,2},{3,19},{19,3},{4,20},{20... | collective-permute-start | bytes 737288 | tf_op jit(solution)/shard_map/ppermute | solution.py:377
  47.5 1.6 %collective-permute-start.7 = (bf16[32,1280]{1,0:T(8,128)(2,1)S(1)}, bf16[32,1280]{1,0:T(8,128)(2,1)S(1)}, u32[]{:S(2)}, u32[]{:S(2)}) collective-permute-start(bf16[32,1280]{1,0:T(8,128)(2,1)S(1)} %collective-permute-done.1.refs_3_), channel_id=1, source_target_pairs={{0,16},{16,0},{1,17},{17,1},{2,18},{18,2},{3,19},{19,3},{4,20},{20... | collective-permute-start | bytes 245768 | tf_op jit(solution)/shard_map/ppermute | solution.py:377
  49.1 0.8 copy-start.11
  49.1 0.7 copy-start.8
  79.7 4.2 %collective-permute-start.9 = (f32[32,64]{1,0:T(8,128)S(1)}, f32[32,64]{1,0:T(8,128)S(1)}, u32[]{:S(2)}, u32[]{:S(2)}) collective-permute-start(f32[32,64]{1,0:T(8,128)S(1)} %get-tuple-element.33.refs_0_.own_ref), channel_id=1, source_target_pairs={{4,0},{8,4},{12,8},{0,12},{5,1},{9,5},{13,9},{1,13},{6,2},{10,6},{... | collective-permute-start | bytes 24584 | tf_op jit(solution)/shard_map/ppermute | solution.py:294
  81.2 3.7 %collective-permute-start.8 = (f32[32,64]{1,0:T(8,128)S(1)}, f32[32,64]{1,0:T(8,128)S(1)}, u32[]{:S(2)}, u32[]{:S(2)}) collective-permute-start(f32[32,64]{1,0:T(8,128)S(1)} %get-tuple-element.33.refs_0_.own_ref), channel_id=1, source_target_pairs={{0,4},{4,8},{8,12},{12,0},{1,5},{5,9},{9,13},{13,1},{2,6},{6,10},{... | collective-permute-start | bytes 24584 | tf_op jit(solution)/shard_map/ppermute | solution.py:294
  83.9 1.6 %copy-start.12 = (f32[384]{0:T(512)S(1)}, f32[384]{0:T(512)}, u32[]{:S(2)}) copy-start(f32[384]{0:T(512)} %param.24) | copy-start | bytes 4612
  83.9 1.6 %copy-start.13 = (f32[384]{0:T(512)S(1)}, f32[384]{0:T(512)}, u32[]{:S(2)}) copy-start(f32[384]{0:T(512)} %param.25) | copy-start | bytes 4612
  83.9 1.6 %copy-start.14 = (f32[384]{0:T(512)S(1)}, f32[384]{0:T(512)}, u32[]{:S(2)}) copy-start(f32[384]{0:T(512)} %param.27) | copy-start | bytes 4612
  84.9 2.9 %collective-permute-start.11 = (f32[4,24,64]{2,1,0:T(8,128)S(1)}, f32[4,24,64]{2,1,0:T(8,128)S(1)}, u32[]{:S(2)}, u32[]{:S(2)}) collective-permute-start(f32[4,24,64]{2,1,0:T(8,128)S(1)} %shard_map.155.refs_0_.refs_1_), channel_id=1, source_target_pairs={{16,0},{32,16},{48,32},{64,48},{80,64},{96,80},{112,96},{128,112},... | collective-permute-start | bytes 73736 | tf_op jit(solution)/shard_map/ppermute | solution.py:294
  85.0 5.7 %collective-permute-start.10 = (f32[4,24,64]{2,1,0:T(8,128)S(1)}, f32[4,24,64]{2,1,0:T(8,128)S(1)}, u32[]{:S(2)}, u32[]{:S(2)}) collective-permute-start(f32[4,24,64]{2,1,0:T(8,128)S(1)} %shard_map.155.refs_0_.refs_1_), channel_id=1, source_target_pairs={{0,16},{16,32},{32,48},{48,64},{64,80},{80,96},{96,112},{112,128},... | collective-permute-start | bytes 73736 | tf_op jit(solution)/shard_map/ppermute | solution.py:294
  85.5 5.2 %copy-start.1 = (bf16[432,384]{1,0:T(8,128)(2,1)S(1)}, bf16[432,384]{1,0:T(8,128)(2,1)}, u32[]{:S(2)}) copy-start(bf16[432,384]{1,0:T(8,128)(2,1)} %refs_3_.1) | copy-start | bytes 995332

commit v2 on v1

--- a/solution.py
+++ b/solution.py
@@ -27,18 +27,16 @@
     )(*args)
 
 
-def pack_kernel(q_ref, k_ref, v_ref, w_ref, out_ref, low_ref, high_ref, inner_ref, held, packed, sems, out_sems):
+def pack_kernel(q_ref, k_ref, v_ref, w_ref, out_ref, low_ref, high_ref, held, packed, sems, out_sems):
     heads = out_ref.shape[0]
-    step = w_ref.shape[0] // (sems.shape[0] - 3)
+    split, depth = low_ref.shape[0], w_ref.shape[0]
+    step = depth // (sems.shape[0] - 3)
     copies = [
         pltpu.make_async_copy(ref, held.at[at], sems.at[at]) for at, ref in enumerate((q_ref, k_ref, v_ref))
     ]
-    taken = 0
-    for ref in (low_ref, high_ref, inner_ref):
-        for row in range(0, ref.shape[0], step):
-            source = w_ref.at[taken + row : taken + row + step]
-            copies.append(pltpu.make_async_copy(source, ref.at[row : row + step], sems.at[len(copies)]))
-        taken += ref.shape[0]
+    for at, row in enumerate(range(0, depth, step)):
+        target = low_ref.at[row : row + step] if row < split else high_ref.at[row - split : row - split + step]
+        copies.append(pltpu.make_async_copy(w_ref.at[row : row + step], target, sems.at[3 + at]))
     for copy in copies:
         copy.start()
     sends = []
@@ -103,13 +101,12 @@
 
 
 def projection_kernel(att_ref, *refs):
-    refs, (out_ref, held, total, sems) = refs[:-4], refs[-4:]
+    refs, (out_ref, held, sems) = refs[:-3], refs[-3:]
     targets, rows, cols = out_ref.shape
     steps, depth, _ = held.shape
     n_x = att_ref.shape[0] // steps
     zl, core = lax.axis_index("zl"), lax.axis_index("core")
-    starts = (0, refs[1].shape[0], refs[1].shape[0] + refs[2].shape[0])
-    layout = ((0, 0), (1, starts[0]), (1, starts[1]), (1, starts[2]))
+    layout = ((0, 0), (1, 0), (1, refs[1].shape[0]))
     copies = [[] for _ in range(steps)]
     for at, ref in enumerate(refs):
         step, start = layout[at % len(layout)]
@@ -119,16 +116,18 @@
     for step in range(steps):
         for copy in copies[step]:
             copy.start()
+    feats = jnp.concatenate(
+        [att_ref[base + x] for base in (zl * n_x, (1 - zl) * n_x) for x in range(n_x)], axis=1
+    )
     for step in range(steps):
-        base = (zl if step == 0 else 1 - zl) * n_x
-        feats = jnp.concatenate([att_ref[base + x] for x in range(n_x)], axis=1)
         for copy in copies[step]:
             copy.wait()
-        term = jnp.dot(feats, held[step], preferred_element_type=F32)
-        if step == 0:
-            total[...] = term
-        else:
-            out_ref[...] = (total[...] + term).astype(BF16).reshape(targets, rows, cols)
+    chunk = 256
+    for start in range(0, cols, chunk):
+        span = slice(start, start + chunk)
+        weight = held[:, :, span].reshape(steps * depth, chunk)
+        terms = jnp.dot(feats, weight, preferred_element_type=F32)
+        out_ref[:, :, span] = terms.astype(BF16).reshape(targets, rows, chunk)
 
 
 def fetch_kernel(skip, after_ref, weight_ref, out_ref, sems):
@@ -154,7 +153,7 @@
         out_shape=pltpu.VMEM((rows, weight.shape[1]), BF16),
         in_specs=[pl.BlockSpec(memory_space=pl.ANY), HBM],
         out_specs=VMEM,
-        scratch_shapes=[pltpu.SemaphoreType.DMA((8,))],
+        scratch_shapes=[pltpu.SemaphoreType.DMA((4,))],
         compiler_params=pltpu.CompilerParams(vmem_limit_bytes=8 * 1024 * 1024),
         cost_estimate=pl.CostEstimate(flops=0, bytes_accessed=4 * rows * weight.shape[1], transcendentals=0),
     )(after, in_hbm(weight))
@@ -281,10 +280,9 @@
         for a in range(2):
             for b in range(2):
                 cell = total[f, a, b] + first[b, f, 1 + a]
-                for n in range(chans // 128):
-                    result[n, f, a, pl.ds(b, cols, stride=2)] = cell[:, 128 * n : 128 * (n + 1)]
-    for n in range(chans // 128):
-        out_ref[:, :, :, 128 * n : 128 * (n + 1)] = result[n].astype(BF16)
+                for c in range(cols):
+                    result[f, a, 2 * c + b : 2 * c + b + 1] = cell[c : c + 1]
+    out_ref[...] = result[...].astype(BF16)
 
 
 def neighbours(block, axis):
@@ -319,12 +317,12 @@
     assert heads == chips
 
     depth, n_cols = out_weight.shape
-    weight_parts = [jax.ShapeDtypeStruct((rows, n_cols), BF16) for rows in (depth * 3 // 8, depth // 2, depth // 8)]
-    packed, weight_low, weight_high, weight_inner = pl.pallas_call(
+    weight_parts = [jax.ShapeDtypeStruct((rows, n_cols), BF16) for rows in (depth * 7 // 16, depth * 9 // 16)]
+    packed, weight_low, weight_high = pl.pallas_call(
         pack_kernel,
         out_shape=(jax.ShapeDtypeStruct((heads, tokens, 3 * HEAD_DIM), BF16), *weight_parts),
         in_specs=[HBM] * 4,
-        out_specs=(HBM, HBM, HBM, HBM),
+        out_specs=(HBM, HBM, HBM),
         scratch_shapes=[
             pltpu.VMEM((3, tokens, features), BF16),
             pltpu.VMEM((3, heads, tokens, HEAD_DIM), BF16),
@@ -340,8 +338,7 @@
         low, high = dp, n_dp + (dp - 1) % n_dp
         outer += [(low, high), (high, low)]
     from_first = lax.ppermute(weight_high, ("zl", "dp"), outer)
-    from_inner = lax.ppermute(weight_inner, "zl", swap)
-    own, from_first, from_inner = lax.optimization_barrier((own, from_first, from_inner))
+    own, from_first = lax.optimization_barrier((own, from_first))
     other = lax.ppermute(own, "core", swap)
     sources = (n_zl * n_y, n_x * tokens, 3 * HEAD_DIM)
     held = n_y * n_x * tokens
@@ -369,29 +366,23 @@
     attended = lax.all_to_all(
         attended_here.reshape(n_zl * n_x, held, HEAD_DIM), ("zl", "tp"), 0, 0, tiled=True
     )
-    weight_low, out_weight, from_first, from_inner, _ = lax.optimization_barrier(
-        (weight_low, out_weight, from_first, from_inner, attended_here)
+    weight_low, out_weight, from_first, _ = lax.optimization_barrier(
+        (weight_low, out_weight, from_first, attended_here)
     )
     from_last = lax.ppermute(weight_low, ("zl", "dp"), outer)
-    near = (out_weight, from_last, from_first, from_inner)
+    near = (out_weight, from_last, from_first)
     far = tuple(lax.ppermute(piece, "core", swap) for piece in near)
     terms = pl.pallas_call(
         projection_kernel,
         out_shape=jax.ShapeDtypeStruct((n_y * n_x, tokens, n_cols), BF16),
-        in_specs=[VMEM] + [HBM] * 5 + [VMEM, HBM, HBM],
+        in_specs=[VMEM] + [HBM] * 6,
         out_specs=VMEM,
         scratch_shapes=[
             pltpu.VMEM((n_zl, 2 * out_weight.shape[0], n_cols), BF16),
-            pltpu.VMEM((held, n_cols), F32),
-            pltpu.SemaphoreType.DMA((8,)),
+            pltpu.SemaphoreType.DMA((6,)),
         ],
         compiler_params=pltpu.CompilerParams(vmem_limit_bytes=24 * 1024 * 1024),
-    )(
-        attended,
-        *[in_hbm(piece) for piece in near + far[:1]],
-        pltpu.with_memory_space_constraint(far[1], pltpu.VMEM),
-        *[in_hbm(piece) for piece in far[2:]],
-    )
+    )(attended, *[in_hbm(piece) for piece in near + far])
     terms = lax.all_to_all(terms, ("y", "tp"), 0, 0, tiled=True)
     patch_width = head_weight.shape[1]
     block_out, patch = call(
@@ -439,7 +430,7 @@
             pltpu.VMEM((2, frames, 4, col_dev, chans), F32),
             pltpu.VMEM((frames, 4, 4, col_dev, chans), F32),
             pltpu.VMEM((128, depth), BF16),
-            pltpu.VMEM((chans // 128, frames, 2, 2 * col_dev, 128), F32),
+            pltpu.VMEM((frames, 2, 2 * col_dev, chans), F32),
         ],
         compiler_params=pltpu.CompilerParams(vmem_limit_bytes=32 * 1024 * 1024),
     )(

time: 94.6 us -> 94.9 us (level)
  waiting for transfers between devices: 20.5 us -> 21.6 us
    ppermute x1, waiting for transfers between devices: 0.79 us -> 8.03 us  [shards(): from_first = lax.ppermute(weight_high, ('zl', 'dp'), outer)]
    ppermute x1 -> x0, waiting for transfers between devices: 6.36 us -> none  [shards(): from_inner = lax.ppermute(weight_inner, 'zl', swap)]
    all_to_all x1, waiting for transfers between devices: 1.16 us -> 0.01 us  [shards(): own = lax.all_to_all(packed, ('zl', 'y', 'tp'), 0, 0, tiled=True)]
  transfers between devices with their start and end apart: 14 -> 12, of which waited for: 8 -> 6; matrix products, arithmetic and copies ran while one was open for 0% -> 0% of each run, Pallas kernels for 6% -> 6%
where the time goes in v2:
time: 94.9 us; the launch traced here: 94.6 us
  starting transfers between devices  27.4 us (29%)
  blocking collectives  24.9 us (26%)
  waiting for transfers between devices  21.6 us (23%)
  Pallas kernels  19 us (20%)
    all_to_all x1, blocking collectives, shards(): terms = lax.all_to_all(terms, ('y', 'tp'), 0, 0, tiled=True)  24.9 us
    all_to_all x1, starting transfers between devices, shards(): own = lax.all_to_all(packed, ('zl', 'y', 'tp'), 0, 0, tiled=True)  8.98 us
    ppermute x1, waiting for transfers between devices, shards(): from_first = lax.ppermute(weight_high, ('zl', 'dp'), outer)  8.03 us
    ppermute x1, waiting for transfers between devices, shards(): from_last = lax.ppermute(weight_low, ('zl', 'dp'), outer)  7.25 us
    ppermute x1, starting transfers between devices, shards(): from_first = lax.ppermute(weight_high, ('zl', 'dp'), outer)  5.5 us
    ppermute x1, starting transfers between devices, shards(): from_last = lax.ppermute(weight_low, ('zl', 'dp'), outer)  5.13 us
    all_to_all x1, starting transfers between devices, shards(): lax.all_to_all(attended_here.reshape(n_zl * n_x, held, HEAD_DIM), ('zl',...  4.81 us
    pallas_call x2, Pallas kernels, fetch(): pl.pallas_call(lambda *refs: fetch_kernel(skip, *refs), out_shape=pltpu.V...  4.32 us
  transfers between devices with their start and end apart: 12, of which 6 were waited for; matrix products, arithmetic and copies ran while one was open for 0% of the time, Pallas kernels for 6%

profile of v2, /device:TPU:2, one launch (start us, length us, event | category | flops | bytes accessed | tf_op | source)
XLA Modules:
  0.0 94.6 jit_solution(13938337178807810286)
XLA Ops:
  0.6 2.1 %shard_map.149 = (bf16[32,32,384]{2,1,0:T(8,128)(2,1)}, bf16[112,1280]{1,0:T(8,128)(2,1)S(1)}, bf16[144,1280]{1,0:T(8,128)(2,1)S(1)}) custom-call(bf16[32,4096]{1,0:T(8,128)(2,1)} %bitcast.22, bf16[32,4096]{1,0:T(8,128)(2,1)} %bitcast.23, bf16[32,4096]{1,0:T(8,128)(2,1)} %bitcast.24, bf16[256,1280]{1,0:T(8,128)(2,1)} %refs_0_), custom_call_target="tpu_custom_call" | custom-call | tf_op jit(solution)/shard_map/pallas_call | solution.py:321
  2.7 9.0 %all-to-all-start = ((bf16[32,32,384]{2,1,0:T(8,128)(2,1)}), bf16[32,32,384]{2,1,0:T(8,128)(2,1)S(1)}, u32[]{:S(2)}, u32[]{:S(2)}) async-start(bf16[32,32,384]{2,1,0:T(8,128)(2,1)} %get-tuple-element.15), calls=%async_computation | async-start | bytes 1572864 | tf_op jit(solution)/shard_map/all_to_all | solution.py:334
  11.7 0.0 copy-start.6
  11.7 5.5 %collective-permute-start = (bf16[144,1280]{1,0:T(8,128)(2,1)S(1)}, bf16[144,1280]{1,0:T(8,128)(2,1)S(1)}, u32[]{:S(2)}, u32[]{:S(2)}) collective-permute-start(bf16[144,1280]{1,0:T(8,128)(2,1)S(1)} %get-tuple-element.16), channel_id=1, source_target_pairs={{0,131},{131,0},{1,128},{128,1},{2,129},{129,2},{3,130},{130,3},{4... | collective-permute-start | bytes 1105928 | tf_op jit(solution)/shard_map/ppermute | solution.py:340
  17.2 8.0 %collective-permute-done.refs_2_ = bf16[144,1280]{1,0:T(8,128)(2,1)S(1)} collective-permute-done((bf16[144,1280]{1,0:T(8,128)(2,1)S(1)}, bf16[144,1280]{1,0:T(8,128)(2,1)S(1)}, u32[]{:S(2)}, u32[]{:S(2)}) %collective-permute-start) | collective-permute-done | bytes 368672 | tf_op jit(solution)/shard_map/ppermute | solution.py:340
  25.3 1.5 %shard_map.150 = (f32[4,256,128]{2,1,0:T(8,128)S(1)}, f32[4,256,1]{2,1,0:T(8,128)S(1)}, f32[4,256,1]{2,1,0:T(8,128)S(1)}) custom-call(bf16[8,128,384]{2,1,0:T(8,128)(2,1)S(1)} %bitcast.14), custom_call_target="tpu_custom_call" | custom-call | bytes 8388608 | tf_op jit(solution)/shard_map/pallas_call | solution.py:20
  26.7 0.8 collective-permute-done.1
  27.6 3.0 %shard_map.151 = bf16[2,4,512,128]{3,2,1,0:T(8,128)(2,1)} custom-call(bf16[8,128,384]{2,1,0:T(8,128)(2,1)S(1)} %bitcast.15, bf16[8,128,384]{2,1,0:T(8,128)(2,1)S(1)} %bitcast.16, f32[4,256,128]{2,1,0:T(8,128)S(1)} %get-tuple-element.18.mixed_ref, f32[4,256,1]{2,1,0:T(8,128)S(1)} %get-tuple-element.19.top_ref, f32[4,256,1]{2,1,0:T(8,128)S(1)} %get-tuple-element.20.total_ref), custom_call_target="tpu_custom_call" | custom-call | tf_op jit(solution)/shard_map/pallas_call | solution.py:355
  30.6 4.8 %all-to-all-start.1 = ((bf16[8,512,128]{2,1,0:T(8,128)(2,1)}), bf16[8,512,128]{2,1,0:T(8,128)(2,1)S(1)}, u32[]{:S(2)}, u32[]{:S(2)}) async-start(bf16[8,512,128]{2,1,0:T(8,128)(2,1)} %bitcast.5), calls=%async_computation.1 | async-start | bytes 2097152 | tf_op jit(solution)/shard_map/all_to_all | solution.py:366
  35.4 0.0 copy-start.4
  35.4 0.0 copy-start.5
  35.4 0.1 collective-permute-start.3
  35.5 5.1 %collective-permute-start.2 = (bf16[112,1280]{1,0:T(8,128)(2,1)S(1)}, bf16[112,1280]{1,0:T(8,128)(2,1)S(1)}, u32[]{:S(2)}, u32[]{:S(2)}) collective-permute-start(bf16[112,1280]{1,0:T(8,128)(2,1)S(1)} %get-tuple-element.24), channel_id=1, source_target_pairs={{0,131},{131,0},{1,128},{128,1},{2,129},{129,2},{3,130},{130,3},{4... | collective-permute-start | bytes 860168 | tf_op jit(solution)/shard_map/ppermute | solution.py:372
  40.6 0.1 collective-permute-start.5
  40.8 7.3 %collective-permute-done.2.refs_1_ = bf16[112,1280]{1,0:T(8,128)(2,1)S(1)} collective-permute-done((bf16[112,1280]{1,0:T(8,128)(2,1)S(1)}, bf16[112,1280]{1,0:T(8,128)(2,1)S(1)}, u32[]{:S(2)}, u32[]{:S(2)}) %collective-permute-start.2) | collective-permute-done | bytes 286752 | tf_op jit(solution)/shard_map/ppermute | solution.py:372
  48.1 1.6 %collective-permute-done.4.refs_4_ = bf16[112,1280]{1,0:T(8,128)(2,1)S(1)} collective-permute-done((bf16[112,1280]{1,0:T(8,128)(2,1)S(1)}, bf16[112,1280]{1,0:T(8,128)(2,1)S(1)}, u32[]{:S(2)}, u32[]{:S(2)}) %collective-permute-start.4) | collective-permute-done | bytes 286752 | tf_op jit(solution)/shard_map/ppermute | solution.py:374
  49.7 0.7 copy-done.10
  50.4 3.2 %shard_map.152 = bf16[16,32,1280]{2,1,0:T(8,128)(2,1)S(1)} custom-call(bf16[8,512,128]{2,1,0:T(8,128)(2,1)S(1)} %all-to-all-done.1.att_ref, bf16[256,1280]{1,0:T(8,128)(2,1)} %refs_0_, bf16[112,1280]{1,0:T(8,128)(2,1)} %copy-done.9, bf16[144,1280]{1,0:T(8,128)(2,1)} %copy-done.7, bf16[256,1280]{1,0:T(8,128)(2,1)} %collective-permute-done.3.refs_3_, ...), custom_call_target="tpu_custom_call" | custom-call | tf_op jit(solution)/shard_map/pallas_call | solution.py:375
  53.6 24.9 %all_to_all.15.refs_0_ = bf16[16,32,1280]{2,1,0:T(8,128)(2,1)S(1)} all-to-all(bf16[16,32,1280]{2,1,0:T(8,128)(2,1)S(1)} %shard_map.152), channel_id=1, replica_groups=mesh['zl'=2,'y'=4,'core'=2,'tp'=4,'dp'=4] {'y','tp'}, dimensions={0} | all-to-all | bytes 2621440 | tf_op jit(solution)/shard_map/all_to_all | solution.py:386
  78.5 1.4 %shard_map.153 = (bf16[32,5120]{1,0:T(8,128)(2,1)}, f32[32,64]{1,0:T(8,128)S(1)}) custom-call(bf16[16,32,1280]{2,1,0:T(8,128)(2,1)S(1)} %all_to_all.15.refs_0_, bf16[32,5120]{1,0:T(8,128)(2,1)S(1)} %bitcast.18, f32[1,5120]{1,0:T(1,128)S(1)} %bitcast.19, f32[1,5120]{1,0:T(1,128)S(1)} %bitcast.20, f32[1,5120]{1,0:T(1,128)S(1)} %bitcast.21, ...), custom_call_target="tpu_custom_call" | custom-call | bytes 16777216 | tf_op jit(solution)/shard_map/pallas_call | solution.py:20
  79.9 1.5 %collective-permute-start.7 = (f32[32,64]{1,0:T(8,128)S(1)}, f32[32,64]{1,0:T(8,128)S(1)}, u32[]{:S(2)}, u32[]{:S(2)}) collective-permute-start(f32[32,64]{1,0:T(8,128)S(1)} %get-tuple-element.27.refs_0_.own_ref), channel_id=1, source_target_pairs={{4,0},{8,4},{12,8},{0,12},{5,1},{9,5},{13,9},{1,13},{6,2},{10,6},{... | collective-permute-start | bytes 24584 | tf_op jit(solution)/shard_map/ppermute | solution.py:292
  81.3 0.6 collective-permute-start.6
  81.9 2.1 %shard_map.154.after_ref.refs_6_ = bf16[5120,384]{1,0:T(8,128)(2,1)S(1)} custom-call(f32[32,64]{1,0:T(8,128)S(1)} %get-tuple-element.27.refs_0_.own_ref, bf16[10368,384]{1,0:T(8,128)(2,1)} %refs_1_.3), custom_call_target="tpu_custom_call" | custom-call | bytes 7864320 | tf_op jit(solution)/shard_map/pallas_call | solution.py:151
  84.0 0.0 copy-start.11
  84.0 0.0 copy-start.12
  84.0 0.0 copy-start.13
  84.1 1.0 %collective-permute-done.6.left_ref = f32[32,64]{1,0:T(8,128)S(1)} collective-permute-done((f32[32,64]{1,0:T(8,128)S(1)}, f32[32,64]{1,0:T(8,128)S(1)}, u32[]{:S(2)}, u32[]{:S(2)}) %collective-permute-start.6) | collective-permute-done | bytes 8224 | tf_op jit(solution)/shard_map/ppermute | solution.py:292
  85.1 0.3 collective-permute-start.9
  85.3 0.5 collective-permute-start.8
  85.9 2.2 %shard_map.156.refs_7_ = bf16[5248,384]{1,0:T(8,128)(2,1)S(1)} custom-call(f32[4,24,64]{2,1,0:T(8,128)S(1)} %shard_map.155.refs_0_.refs_1_, bf16[10368,384]{1,0:T(8,128)(2,1)} %refs_1_.3), custom_call_target="tpu_custom_call" | custom-call | bytes 8060928 | tf_op jit(solution)/shard_map/pallas_call | solution.py:151
  88.1 2.9 %collective-permute-done.8.refs_0_ = f32[4,24,64]{2,1,0:T(8,128)S(1)} collective-permute-done((f32[4,24,64]{2,1,0:T(8,128)S(1)}, f32[4,24,64]{2,1,0:T(8,128)S(1)}, u32[]{:S(2)}, u32[]{:S(2)}) %collective-permute-start.8) | collective-permute-done | bytes 24608 | tf_op jit(solution)/shard_map/ppermute | solution.py:292
  91.0 3.5 %shard_map.157 = bf16[4,2,16,384]{3,2,1,0:T(8,128)(2,1)} custom-call(f32[4,24,64]{2,1,0:T(8,128)S(1)} %collective-permute-done.8.refs_0_, f32[4,24,64]{2,1,0:T(8,128)S(1)} %shard_map.155.refs_0_.refs_1_, f32[4,24,64]{2,1,0:T(8,128)S(1)} %collective-permute-done.9.refs_2_, bf16[432,384]{1,0:T(8,128)(2,1)S(1)} %copy-done.1, f32[1,384]{1,0:T(1,128)S(1)} %reshape.57.refs_4_, ...), custom_call_target="tpu_custom_call" | custom-call | tf_op jit(solution)/shard_map/pallas_call | solution.py:421
  (33 shorter events, 0.1 us)
Async XLA Ops:
  2.7 22.5 %all-to-all-start = ((bf16[32,32,384]{2,1,0:T(8,128)(2,1)}), bf16[32,32,384]{2,1,0:T(8,128)(2,1)S(1)}, u32[]{:S(2)}, u32[]{:S(2)}) async-start(bf16[32,32,384]{2,1,0:T(8,128)(2,1)} %get-tuple-element.15), calls=%async_computation | async-start | bytes 1572864 | tf_op jit(solution)/shard_map/all_to_all | solution.py:334
  11.7 23.7 %copy-start.6 = (bf16[256,1280]{1,0:T(8,128)(2,1)S(1)}, bf16[256,1280]{1,0:T(8,128)(2,1)}, u32[]{:S(2)}) copy-start(bf16[256,1280]{1,0:T(8,128)(2,1)} %refs_0_) | copy-start | bytes 1966084
  11.7 13.5 %collective-permute-start = (bf16[144,1280]{1,0:T(8,128)(2,1)S(1)}, bf16[144,1280]{1,0:T(8,128)(2,1)S(1)}, u32[]{:S(2)}, u32[]{:S(2)}) collective-permute-start(bf16[144,1280]{1,0:T(8,128)(2,1)S(1)} %get-tuple-element.16), channel_id=1, source_target_pairs={{0,131},{131,0},{1,128},{128,1},{2,129},{129,2},{3,130},{130,3},{4... | collective-permute-start | bytes 1105928 | tf_op jit(solution)/shard_map/ppermute | solution.py:340
  25.3 24.4 %copy-start.7 = (bf16[144,1280]{1,0:T(8,128)(2,1)}, bf16[144,1280]{1,0:T(8,128)(2,1)S(1)}, u32[]{:S(2)}) copy-start(bf16[144,1280]{1,0:T(8,128)(2,1)S(1)} %collective-permute-done.refs_2_) | copy-start | bytes 1105924
  25.3 2.3 %collective-permute-start.1 = (bf16[32,32,384]{2,1,0:T(8,128)(2,1)S(1)}, bf16[32,32,384]{2,1,0:T(8,128)(2,1)S(1)}, u32[]{:S(2)}, u32[]{:S(2)}) collective-permute-start(bf16[32,32,384]{2,1,0:T(8,128)(2,1)S(1)} %all-to-all-done), channel_id=1, source_target_pairs={{0,16},{16,0},{1,17},{17,1},{2,18},{18,2},{3,19},{19,3},{4,20},{20... | collective-permute-start | bytes 2359304 | tf_op jit(solution)/shard_map/ppermute | solution.py:342
  30.6 19.1 %all-to-all-start.1 = ((bf16[8,512,128]{2,1,0:T(8,128)(2,1)}), bf16[8,512,128]{2,1,0:T(8,128)(2,1)S(1)}, u32[]{:S(2)}, u32[]{:S(2)}) async-start(bf16[8,512,128]{2,1,0:T(8,128)(2,1)} %bitcast.5), calls=%async_computation.1 | async-start | bytes 2097152 | tf_op jit(solution)/shard_map/all_to_all | solution.py:366
  35.4 43.1 %copy-start = (bf16[5120,64]{0,1:T(8,128)(2,1)S(1)}, bf16[5120,64]{0,1:T(8,128)(2,1)}, u32[]{:S(2)}) copy-start(bf16[5120,64]{0,1:T(8,128)(2,1)} %param.22) | copy-start | bytes 1966084
  35.4 43.1 %copy-start.2 = (bf16[4,1,8,5120]{3,2,1,0:T(8,128)(2,1)S(1)}, bf16[4,1,8,5120]{3,2,1,0:T(8,128)(2,1)}, u32[]{:S(2)}) copy-start(bf16[4,1,8,5120]{3,2,1,0:T(8,128)(2,1)} %param.17) | copy-start | bytes 983044
  35.4 43.1 %copy-start.3 = (f32[5120]{0:T(1024)S(1)}, f32[5120]{0:T(1024)}, u32[]{:S(2)}) copy-start(f32[5120]{0:T(1024)} %param.19) | copy-start | bytes 61444
  35.4 43.1 %copy-start.4 = (f32[5120]{0:T(1024)S(1)}, f32[5120]{0:T(1024)}, u32[]{:S(2)}) copy-start(f32[5120]{0:T(1024)} %param.20) | copy-start | bytes 61444
  35.4 43.1 %copy-start.5 = (f32[5120]{0:T(1024)S(1)}, f32[5120]{0:T(1024)}, u32[]{:S(2)}) copy-start(f32[5120]{0:T(1024)} %param.21) | copy-start | bytes 61444
  35.4 14.2 %collective-permute-start.3 = (bf16[256,1280]{1,0:T(8,128)(2,1)S(1)}, bf16[256,1280]{1,0:T(8,128)(2,1)}, u32[]{:S(2)}, u32[]{:S(2)}) collective-permute-start(bf16[256,1280]{1,0:T(8,128)(2,1)S(1)} %copy-done.6), channel_id=1, source_target_pairs={{0,16},{16,0},{1,17},{17,1},{2,18},{18,2},{3,19},{19,3},{4,20},{20... | collective-permute-start | bytes 1966088 | tf_op jit(solution)/shard_map/ppermute | solution.py:374
  35.5 12.5 %collective-permute-start.2 = (bf16[112,1280]{1,0:T(8,128)(2,1)S(1)}, bf16[112,1280]{1,0:T(8,128)(2,1)S(1)}, u32[]{:S(2)}, u32[]{:S(2)}) collective-permute-start(bf16[112,1280]{1,0:T(8,128)(2,1)S(1)} %get-tuple-element.24), channel_id=1, source_target_pairs={{0,131},{131,0},{1,128},{128,1},{2,129},{129,2},{3,130},{130,3},{4... | collective-permute-start | bytes 860168 | tf_op jit(solution)/shard_map/ppermute | solution.py:372
  40.6 7.4 %collective-permute-start.5 = (bf16[144,1280]{1,0:T(8,128)(2,1)S(1)}, bf16[144,1280]{1,0:T(8,128)(2,1)S(1)}, u32[]{:S(2)}, u32[]{:S(2)}) collective-permute-start(bf16[144,1280]{1,0:T(8,128)(2,1)S(1)} %collective-permute-done.refs_2_), channel_id=1, source_target_pairs={{0,16},{16,0},{1,17},{17,1},{2,18},{18,2},{3,19},{19,3},{4,20},{20... | collective-permute-start | bytes 1105928 | tf_op jit(solution)/shard_map/ppermute | solution.py:374
  48.0 1.6 %copy-start.9 = (bf16[112,1280]{1,0:T(8,128)(2,1)}, bf16[112,1280]{1,0:T(8,128)(2,1)S(1)}, u32[]{:S(2)}) copy-start(bf16[112,1280]{1,0:T(8,128)(2,1)S(1)} %collective-permute-done.2.refs_1_) | copy-start | bytes 860164
  48.0 1.6 %collective-permute-start.4 = (bf16[112,1280]{1,0:T(8,128)(2,1)S(1)}, bf16[112,1280]{1,0:T(8,128)(2,1)S(1)}, u32[]{:S(2)}, u32[]{:S(2)}) collective-permute-start(bf16[112,1280]{1,0:T(8,128)(2,1)S(1)} %collective-permute-done.2.refs_1_), channel_id=1, source_target_pairs={{0,16},{16,0},{1,17},{17,1},{2,18},{18,2},{3,19},{19,3},{4,20},{20... | collective-permute-start | bytes 860168 | tf_op jit(solution)/shard_map/ppermute | solution.py:374
  48.1 1.6 %copy-start.8 = (bf16[144,1280]{1,0:T(8,128)(2,1)}, bf16[144,1280]{1,0:T(8,128)(2,1)S(1)}, u32[]{:S(2)}) copy-start(bf16[144,1280]{1,0:T(8,128)(2,1)S(1)} %collective-permute-done.5.refs_5_) | copy-start | bytes 1105924
  49.6 0.7 copy-start.10
  79.9 4.2 %collective-permute-start.7 = (f32[32,64]{1,0:T(8,128)S(1)}, f32[32,64]{1,0:T(8,128)S(1)}, u32[]{:S(2)}, u32[]{:S(2)}) collective-permute-start(f32[32,64]{1,0:T(8,128)S(1)} %get-tuple-element.27.refs_0_.own_ref), channel_id=1, source_target_pairs={{4,0},{8,4},{12,8},{0,12},{5,1},{9,5},{13,9},{1,13},{6,2},{10,6},{... | collective-permute-start | bytes 24584 | tf_op jit(solution)/shard_map/ppermute | solution.py:292
  81.3 3.7 %collective-permute-start.6 = (f32[32,64]{1,0:T(8,128)S(1)}, f32[32,64]{1,0:T(8,128)S(1)}, u32[]{:S(2)}, u32[]{:S(2)}) collective-permute-start(f32[32,64]{1,0:T(8,128)S(1)} %get-tuple-element.27.refs_0_.own_ref), channel_id=1, source_target_pairs={{0,4},{4,8},{8,12},{12,0},{1,5},{5,9},{9,13},{13,1},{2,6},{6,10},{... | collective-permute-start | bytes 24584 | tf_op jit(solution)/shard_map/ppermute | solution.py:292
  84.0 1.8 %copy-start.11 = (f32[384]{0:T(512)S(1)}, f32[384]{0:T(512)}, u32[]{:S(2)}) copy-start(f32[384]{0:T(512)} %param.24) | copy-start | bytes 4612
  84.0 1.8 %copy-start.12 = (f32[384]{0:T(512)S(1)}, f32[384]{0:T(512)}, u32[]{:S(2)}) copy-start(f32[384]{0:T(512)} %param.25) | copy-start | bytes 4612
  84.0 1.8 %copy-start.13 = (f32[384]{0:T(512)S(1)}, f32[384]{0:T(512)}, u32[]{:S(2)}) copy-start(f32[384]{0:T(512)} %param.27) | copy-start | bytes 4612
  85.1 3.0 %collective-permute-start.9 = (f32[4,24,64]{2,1,0:T(8,128)S(1)}, f32[4,24,64]{2,1,0:T(8,128)S(1)}, u32[]{:S(2)}, u32[]{:S(2)}) collective-permute-start(f32[4,24,64]{2,1,0:T(8,128)S(1)} %shard_map.155.refs_0_.refs_1_), channel_id=1, source_target_pairs={{16,0},{32,16},{48,32},{64,48},{80,64},{96,80},{112,96},{128,112},... | collective-permute-start | bytes 73736 | tf_op jit(solution)/shard_map/ppermute | solution.py:292
  85.3 5.7 %collective-permute-start.8 = (f32[4,24,64]{2,1,0:T(8,128)S(1)}, f32[4,24,64]{2,1,0:T(8,128)S(1)}, u32[]{:S(2)}, u32[]{:S(2)}) collective-permute-start(f32[4,24,64]{2,1,0:T(8,128)S(1)} %shard_map.155.refs_0_.refs_1_), channel_id=1, source_target_pairs={{0,16},{16,32},{32,48},{48,64},{64,80},{80,96},{96,112},{112,128},... | collective-permute-start | bytes 73736 | tf_op jit(solution)/shard_map/ppermute | solution.py:292
  85.9 5.2 %copy-start.1 = (bf16[432,384]{1,0:T(8,128)(2,1)S(1)}, bf16[432,384]{1,0:T(8,128)(2,1)}, u32[]{:S(2)}) copy-start(bf16[432,384]{1,0:T(8,128)(2,1)} %refs_3_.1) | copy-start | bytes 995332
